TPU v7x, 128 devices: a whole 4x4x4 slice. The times are simulated.
128 devices in a mesh: fsdp: 2 (over x_hi), ctx: 64 (over x_lo, y, z, core).
Axes of the slice: x: 4 (x_hi: 2, x_lo: 2; x = x_hi * 2 + x_lo), y: 4, z: 4, core: 2. Of those that a mesh axis runs over, the one named last changes fastest.
Arguments:
- inputs: bfloat16 [2, 8192, 960], P('fsdp', 'ctx'), may hold values from -6 to 6
- cotangent: bfloat16 [2, 8192, 960], P('fsdp', 'ctx'), may hold values from -6 to 6
- positions: int32 [2, 8192], P('fsdp', 'ctx'), may hold values from 0 to 16382, as said below
- pair_index: int32 [2, 64], P('fsdp', 'ctx'), may hold values from 0 to 63, as said below
- input_projection: bfloat16 [960, 1600], P('ctx', 'fsdp'), may hold values from -0.1875 to 0.1875
- project_out: bfloat16 [960, 960], P('ctx', 'fsdp'), may hold values from -0.75 to 0.75
- gate_up: bfloat16 [960, 2, 2560], P('ctx', None, 'fsdp'), may hold values from -0.1875 to 0.1875
- down_weight: bfloat16 [960, 2560], P('ctx', 'fsdp'), may hold values from -0.125 to 0.125
- norm_gains: bfloat16 [960, 2], P('ctx', 'fsdp'), may hold values from 0.25 to 1.75
Outputs:
- layer_out: bfloat16 [2, 8192, 960], P('fsdp', 'ctx')
- input_grad: bfloat16 [2, 8192, 960], P('fsdp', 'ctx')
- grad_project_in: float32 [960, 1600], P('ctx', 'fsdp')
- grad_project_out: float32 [960, 960], P('ctx', 'fsdp')
- grad_gate_up: float32 [960, 2, 2560], P('ctx', None, 'fsdp')
- grad_down: float32 [960, 2560], P('ctx', 'fsdp')
- grad_gains: float32 [960, 2], P('ctx', 'fsdp')
Inputs may be any that keep to these rules, and one draw needn't show every extreme that they name: Each row is a permutation of 0 to 64 - 1; device c of a sequence holds block pair_index and block 2 * 64 - 1 - pair_index, each of 64 tokens in order. Taken in the causal order that pair_index gives, a sequence's positions start at 0, rise by 1 to 3 from token to token and end at 16382.
All inputs are finite; a program needn't handle non-finite values.
Results may differ from a plain program's by a relative error of at most 0.029.
Values may be sent and summed in bfloat16 or wider, within the bound.
A program may use at most 192 MiB of HBM per device.

v0:
```python
import math

import jax
import jax.numpy as jnp
import numpy as np
from jax import lax
from jax.experimental import pallas as pl
from jax.experimental.pallas import tpu as pltpu
from jax.sharding import PartitionSpec as P

WIDTH = 960
QUERY_HEADS = 15
KEY_VALUE_HEADS = 5
GROUP = 3
HEAD_SIZE = 64
FF_HALF = 1280
FF_QUARTER = 640
EPSILON = 1e-05
ROWS = 16
PADDED = 1024
IN_HALF = 800
IN_PAD = 896
OUT_HALF = 480
OUT_PAD = 512
IN_COLS = 2 * IN_PAD
TILE = 512
QROWS = 384
MESH = pl.DeviceIdType.MESH
VMEM_LIMIT = 56 * 1024 * 1024


def column_map():
    cols = np.full((64, ROWS), -1, np.int32)
    cols[:, :15] = np.arange(64)[:, None] * 15 + np.arange(15)[None, :]
    return cols.reshape(-1)


COLUMN_MAP = column_map()


def coordinates():
    index = lax.axis_index("ctx")
    core = index % 2
    z = (index // 2) % 4
    y = (index // 8) % 4
    x = index // 32
    p1 = y * (1 - core) + z * core
    p2 = z * (1 - core) + y * core
    return x, p1, p2, core


def device_at(x, p1, p2, core):
    y = p1 * (1 - core) + p2 * core
    z = p2 * (1 - core) + p1 * core
    return ((x * 4 + y) * 4 + z) * 2 + core


def neighbours(x, p1, p2, core):
    index = lax.axis_index("ctx")
    return (
        device_at(1 - x, p1, p2, core),
        device_at(x, (p1 + 1) % 4, p2, core),
        device_at(x, (p1 + 3) % 4, p2, core),
        device_at(x, p1, (p2 + 1) % 4, core),
        device_at(x, p1, (p2 + 3) % 4, core),
        index + 1 - 2 * core,
    )


def block_of(ref, core, x, p1, p2):
    return ref.at[x, p1, p2, core] if core == 0 else ref.at[x, p2, p1, core]


def half_of(ref, core, x, p2):
    every = pl.ds(0, 4)
    return ref.at[x, every, p2, core] if core == 0 else ref.at[x, p2, every, core]


def slab_of(ref, core, p2):
    every = pl.ds(0, 4)
    both = pl.ds(0, 2)
    return ref.at[both, every, p2, core] if core == 0 else ref.at[both, p2, every, core]


def row_place():
    return lax.axis_index("fsdp") * 2 + lax.axis_index("ctx") // 32


def row_device(place):
    index = lax.axis_index("ctx")
    return {"fsdp": place // 2, "ctx": (place % 2) * 32 + index % 32}


def ctx_device(index):
    return {"ctx": index}


class Sender:
    def __init__(self, send_sem, recv_sem):
        self.send_sem, self.recv_sem, self.sent = send_sem, recv_sem, []

    def __call__(self, source, place, device):
        number = len(self.sent)
        copy = pltpu.make_async_remote_copy(
            src_ref=source,
            dst_ref=place,
            send_sem=self.send_sem.at[number],
            recv_sem=self.recv_sem.at[number],
            device_id=device,
            device_id_type=MESH,
        )
        copy.start()
        self.sent.append(copy)
        return copy

    def finish(self):
        for copy in self.sent:
            copy.wait_send()


class RowGather:
    def __init__(self, in_ref, out_ref, local_sem, send):
        self.out, self.send = out_ref, send
        here = row_place()
        self.left, self.right = (here + 3) % 4, (here + 1) % 4
        self.local = pltpu.make_async_copy(in_ref, out_ref.at[here], local_sem)
        self.local.start()
        self.from_left = send(in_ref, out_ref.at[here], row_device(self.right))
        self.from_right = send(in_ref, out_ref.at[here], row_device(self.left))

    def forward(self):
        rows = self.out.shape[1] // 2
        low, high = pl.ds(0, rows), pl.ds(rows, rows)
        self.from_left.wait_recv()
        place = self.out.at[self.left, low]
        self.far_low = self.send(place, place, row_device(self.right))
        self.from_right.wait_recv()
        place = self.out.at[self.right, high]
        self.far_high = self.send(place, place, row_device(self.left))

    def finish(self):
        self.far_low.wait_recv()
        self.far_high.wait_recv()
        self.local.wait()


class RowScatter:
    def __init__(self, in_ref, far, near_left, near_right, stage, send):
        self.p, self.far, self.stage, self.send = in_ref, far, stage, send
        self.near_left, self.near_right = near_left, near_right
        self.here = row_place()
        self.left, self.right = (self.here + 3) % 4, (self.here + 1) % 4
        to_left, to_right = row_device(self.left), row_device(self.right)
        opposite = (self.here + 2) % 4
        rows = in_ref.shape[1] // 2
        self.low, self.high = pl.ds(0, rows), pl.ds(rows, rows)
        low, high = self.low, self.high
        self.got_low = send(in_ref.at[opposite, low], far.at[0], to_right)
        self.got_high = send(in_ref.at[opposite, high], far.at[1], to_left)
        self.waits = [
            send(in_ref.at[self.right, high], near_left.at[high], to_right),
            send(in_ref.at[self.left, low], near_right.at[low], to_left),
        ]

    def forward(self):
        rows = self.p.shape[1] // 2
        self.got_low.wait_recv()
        self.stage[0] = self.p[self.right, 0:rows] + self.far[0]
        self.waits.append(
            self.send(self.stage.at[0], self.near_left.at[self.low], row_device(self.right))
        )
        self.got_high.wait_recv()
        self.stage[1] = self.p[self.left, rows : 2 * rows] + self.far[1]
        self.waits.append(
            self.send(self.stage.at[1], self.near_right.at[self.high], row_device(self.left))
        )

    def finish(self, out_ref):
        for copy in self.waits:
            copy.wait_recv()
        total = self.p[self.here].astype(jnp.float32) + self.near_left[...].astype(jnp.float32)
        out_ref[...] = total + self.near_right[...].astype(jnp.float32)


def greet(devices):
    barrier = pltpu.get_barrier_semaphore()
    for device in devices:
        pl.semaphore_signal(barrier, inc=1, device_id=device, device_id_type=MESH)
    pl.semaphore_wait(barrier, len(devices))


def greet_ctx(with_row):
    devices = [ctx_device(index) for index in neighbours(*coordinates())]
    if with_row:
        here = row_place()
        step = 2 * (here % 2) - 1
        devices.append(row_device((here + step + 4) % 4))
    greet(devices)


def row_kernel_entry():
    here = row_place()
    greet([row_device((here + 3) % 4), row_device((here + 1) % 4)])


def row_scratch(rows, columns):
    return [
        pltpu.VMEM((2, rows // 2, columns), jnp.bfloat16),
        pltpu.VMEM((rows, columns), jnp.bfloat16),
        pltpu.VMEM((rows, columns), jnp.bfloat16),
        pltpu.VMEM((2, rows // 2, columns), jnp.bfloat16),
        pltpu.SemaphoreType.DMA((6,)),
        pltpu.SemaphoreType.DMA((6,)),
    ]


class Group:
    def __init__(self, copies):
        self.copies = copies

    def wait_recv(self):
        for copy in self.copies:
            copy.wait_recv()


def gather_kernel(modes, with_row, *refs):
    count = len(modes)
    ins, refs = refs[: count + with_row], refs[count + with_row :]
    outs, refs = refs[: count + with_row], refs[count + with_row :]
    greet_ctx("row" in modes or with_row)
    core = coordinates()[3]
    for chosen in range(2):

        @pl.when(core == chosen)
        def _(chosen=chosen):
            gather_body(chosen, modes, with_row, ins, outs, *refs)


def gather_body(
    core, modes, with_row, ins, outs, local_sem, send_sem, recv_sem, row_local, row_send, row_recv
):
    x, p1, p2, _ = coordinates()
    across, right1, left1, right2, left2, sibling = neighbours(x, p1, p2, core)
    p1p, p1m = (p1 + 1) % 4, (p1 + 3) % 4
    p2p, p2m, p2o = (p2 + 1) % 4, (p2 + 3) % 4, (p2 + 2) % 4
    place = row_place()
    row_left, row_right = (place + 3) % 4, (place + 1) % 4
    sender = Sender(send_sem, recv_sem)
    arrays = range(len(modes))
    plain = [k for k in arrays if modes[k] != "row"]
    rows = [k for k in arrays if modes[k] == "row"]
    mine = [ins[k].at[x] if modes[k] == "split" else ins[k] for k in arrays]
    yours = [ins[k].at[1 - x] if modes[k] == "split" else ins[k] for k in arrays]

    def send(places, to, chosen=arrays, sources=None):
        sources = places if sources is None else sources
        return Group([sender(sources[k], places[k], ctx_device(to)) for k in chosen])

    def block(side, q1):
        return [block_of(outs[k], core, side, q1, p2) for k in arrays]

    def half(side, q2):
        return [half_of(outs[k], core, side, q2) for k in arrays]

    def slot(k, owner):
        width = ins[k].shape[-1]
        columns = pl.ds(pl.multiple_of((owner // 2) * width, 128), width)
        return block_of(outs[k], core, owner % 2, p1, p2).at[pl.ds(0, ROWS), columns]

    here = block(x, p1)
    there = block(1 - x, p1)
    locals_ = [
        pltpu.make_async_copy(
            mine[k], slot(k, place) if k in rows else here[k], local_sem.at[k]
        )
        for k in arrays
    ]
    for copy in locals_:
        copy.start()
    row_near = Group(
        [
            sender(ins[k], slot(k, place), row_device(to))
            for to in (row_right, row_left)
            for k in rows
        ]
    )
    crossed = send(here, across, plain, yours)
    own_left = send(here, right1, plain, mine)
    own_right = send(here, left1, plain, mine)
    row_near.wait_recv()
    row_far = Group(
        [sender(slot(k, row_left), slot(k, row_left), row_device(row_right)) for k in rows]
    )
    crossed.wait_recv()
    other_left = send(there, right1)
    other_right = send(there, left1)
    for copy in locals_:
        copy.wait()
    row_far.wait_recv()
    own_left.copies += send(here, right1, rows).copies
    own_right.copies += send(here, left1, rows).copies
    if with_row:
        row_sender = Sender(row_send, row_recv)
        row = RowGather(ins[-1], outs[-1], row_local, row_sender)
    own_left.wait_recv()
    own_far = send(block(x, p1m), right1)
    own_right.wait_recv()
    own_far.wait_recv()
    own_left = send(half(x, p2), right2)
    own_right = send(half(x, p2), left2)
    last = [send(half(x, p2), sibling)]
    other_right.wait_recv()
    other_far = send(block(1 - x, p1p), left1)
    other_left.wait_recv()
    other_far.wait_recv()
    other_right = send(half(1 - x, p2), left2)
    other_left = send(half(1 - x, p2), right2)
    last.append(send(half(1 - x, p2), sibling))
    own_left.wait_recv()
    own_far = send(half(x, p2m), right2)
    last.append(send(half(x, p2m), sibling))
    own_right.wait_recv()
    last.append(send(half(x, p2p), sibling))
    if with_row:
        row.forward()
    other_right.wait_recv()
    other_far = send(half(1 - x, p2p), left2)
    last.append(send(half(1 - x, p2p), sibling))
    other_left.wait_recv()
    last.append(send(half(1 - x, p2m), sibling))
    own_far.wait_recv()
    last.append(send(half(x, p2o), sibling))
    if with_row:
        row.finish()
    other_far.wait_recv()
    last.append(send(half(1 - x, p2o), sibling))
    for group in last:
        group.wait_recv()
    sender.finish()
    if with_row:
        row_sender.finish()


def gather_blocks(blocks, modes, row_block, collective_id):
    with_row = row_block is not None
    operands = list(blocks)
    shapes = [
        jax.ShapeDtypeStruct(
            (2, 4, 4, 2, block.shape[-2], block.shape[-1] * (2 if mode == "row" else 1)),
            block.dtype,
        )
        for block, mode in zip(blocks, modes)
    ]
    if with_row:
        operands.append(row_block)
        shapes.append(jax.ShapeDtypeStruct((4,) + row_block.shape, row_block.dtype))
    number = 23 * len(blocks)
    return pl.pallas_call(
        lambda *refs: gather_kernel(modes, int(with_row), *refs),
        out_shape=tuple(shapes),
        in_specs=[pl.BlockSpec(memory_space=pl.ANY)] * len(operands),
        out_specs=(pl.BlockSpec(memory_space=pl.ANY),) * len(operands),
        scratch_shapes=[
            pltpu.SemaphoreType.DMA((len(blocks),)),
            pltpu.SemaphoreType.DMA((number,)),
            pltpu.SemaphoreType.DMA((number,)),
            pltpu.SemaphoreType.DMA,
            pltpu.SemaphoreType.DMA((4,)),
            pltpu.SemaphoreType.DMA((4,)),
        ],
        compiler_params=pltpu.CompilerParams(
            collective_id=collective_id, has_side_effects=True
        ),
    )(*operands)


def scatter_kernel(pieces, halved, with_row, side, *refs):
    count = 1 + max(piece[0] for piece in pieces)
    ins, refs = refs[:count], refs[count:]
    if with_row:
        row_in, refs = refs[0], refs[1:]
    side_work, side_in, side_out = side
    side_ins, refs = refs[:side_in], refs[side_in:]
    results = 5 if halved else 1
    out_refs, refs = refs[:results], refs[results:]
    if with_row:
        row_out, refs = refs[0], refs[1:]
    side_outs, refs = refs[:side_out], refs[side_out:]
    (acc, other, far_low, far_high, near_left, near_right) = refs[:6]
    (pair_low, pair_high, pair_left, pair_right, last) = refs[6:11]
    (local_sem, cross_send, cross_recv, send_sem, recv_sem) = refs[11:16]
    x, p1, p2, core = coordinates()
    across, right1, left1, right2, left2, sibling = neighbours(x, p1, p2, core)
    greet_ctx(with_row or halved)
    p1p, p1m, p1o = (p1 + 1) % 4, (p1 + 3) % 4, (p1 + 2) % 4
    p2p, p2m, p2o = (p2 + 1) % 4, (p2 + 3) % 4, (p2 + 2) % 4
    needed = (p2o, p2m, p2p, p2)
    theirs = (p1o, p1m, p1p, p1)
    sender = Sender(send_sem, recv_sem)

    def part(ref, place, piece):
        if len(pieces) == 1:
            return ref.at[place]
        every = [pl.ds(0, size) for size in ref.shape[1:-1]]
        return ref.at[tuple([place] + every + [pl.ds(pieces[piece][3], pieces[piece][2])])]

    def source_of(piece, chosen, place):
        array, start, width, _ = pieces[piece]
        slab = slab_of(ins[array], chosen, place)
        if len(pieces) == 1:
            return slab
        every = [pl.ds(0, size) for size in slab.shape[:-1]]
        return slab.at[tuple(every + [pl.ds(start, width)])]

    def crossing(k, piece, source):
        return pltpu.make_async_remote_copy(
            src_ref=source,
            dst_ref=part(other, theirs[k], piece),
            send_sem=cross_send.at[k, piece],
            recv_sem=cross_recv.at[k, piece],
            device_id=ctx_device(sibling),
            device_id_type=MESH,
        )

    for chosen in range(2):

        @pl.when(core == chosen)
        def _(chosen=chosen):
            for k in range(4):
                for piece in range(len(pieces)):
                    crossing(k, piece, source_of(piece, 1 - chosen, theirs[k])).start()
                    pltpu.make_async_copy(
                        source_of(piece, chosen, needed[k]),
                        part(acc, needed[k], piece),
                        local_sem.at[k, piece],
                    ).start()

    if with_row:
        row_sender = Sender(refs[20], refs[21])
        row = RowScatter(row_in, refs[16], refs[17], refs[18], refs[19], row_sender)

    def send(source, place, to):
        return sender(source, place, ctx_device(to))

    def add(place, term):
        @pl.loop(0, 4)
        def _(step):
            place[step] = place[step] + term[step]

    def add_both(side):
        @pl.loop(0, 4)
        def _(step):
            total = acc[p2, side, step].astype(jnp.float32)
            total = total + near_left[side, step].astype(jnp.float32)
            total = total + near_right[side, step].astype(jnp.float32)
            acc[p2, side, step] = total.astype(acc.dtype)

    def merge(k):
        for piece in range(len(pieces)):
            mine = part(acc, needed[k], piece)
            pltpu.make_async_copy(mine, mine, local_sem.at[k, piece]).wait()
            crossing(k, piece, part(other, theirs[k], piece)).wait_recv()
        for side in range(2):
            add(acc.at[needed[k], side], other.at[needed[k], side])

    merge(0)
    got_low = send(acc.at[p2o, 0], far_low, right2)
    got_high = send(acc.at[p2o, 1], far_high, left2)
    merge(1)
    right_low = send(acc.at[p2m, 0], near_right.at[0], left2)
    merge(2)
    left_high = send(acc.at[p2p, 1], near_left.at[1], right2)
    side_work(side_ins, side_outs)
    got_low.wait_recv()
    add(acc.at[p2p, 0], far_low)
    left_low = send(acc.at[p2p, 0], near_left.at[0], right2)
    got_high.wait_recv()
    add(acc.at[p2m, 1], far_high)
    right_high = send(acc.at[p2m, 1], near_right.at[1], left2)
    merge(3)
    if with_row:
        row.forward()
    right_low.wait_recv()
    left_low.wait_recv()
    add_both(0)
    got_low = send(acc.at[p2, 0, p1o], pair_low, right1)
    near_low = send(acc.at[p2, 0, p1m], pair_right.at[0], left1)
    left_high.wait_recv()
    right_high.wait_recv()
    add_both(1)
    got_high = send(acc.at[p2, 1, p1o], pair_high, left1)
    near_high = send(acc.at[p2, 1, p1p], pair_left.at[1], right1)
    got_low.wait_recv()
    acc[p2, 0, p1p] = acc[p2, 0, p1p] + pair_low[...]
    left_low = send(acc.at[p2, 0, p1p], pair_left.at[0], right1)
    got_high.wait_recv()
    acc[p2, 1, p1m] = acc[p2, 1, p1m] + pair_high[...]
    right_high = send(acc.at[p2, 1, p1m], pair_right.at[1], left1)
    if with_row:
        row.finish(row_out)
    near_low.wait_recv()
    near_high.wait_recv()
    left_low.wait_recv()
    right_high.wait_recv()

    @pl.loop(0, 2)
    def _(j):
        total = acc[p2, j, p1].astype(jnp.float32) + pair_left[j].astype(jnp.float32)
        total = total + pair_right[j].astype(jnp.float32)
        acc[p2, j, p1] = total.astype(acc.dtype)

    if halved:
        finish_row(halved, acc, p1, p2, refs[16:20], last, sender, out_refs)
    else:
        final = send(acc.at[p2, 1 - x, p1], last, across)
        final.wait_recv()
        total = acc[p2, x, p1].astype(jnp.float32) + last[...].astype(jnp.float32)
        out_refs[0][...] = total
    for k in range(4):
        for piece in range(len(pieces)):
            crossing(k, piece, part(other, theirs[k], piece)).wait_send()
    sender.finish()
    if with_row:
        row_sender.finish()


def finish_row(halved, acc, p1, p2, buffers, last, sender, out_refs):
    in_ref, out_ref, gu_ref, down_ref, spare_ref = out_refs
    far, from_left, from_right, stage = buffers
    here = row_place()
    left, right, opposite = (here + 3) % 4, (here + 1) % 4, (here + 2) % 4
    x = here % 2
    every = pl.ds(0, ROWS)
    rest = pl.ds(2 * halved, acc.shape[-1] - 2 * halved)

    def columns(owner):
        return pl.ds(pl.multiple_of((owner // 2) * halved, 128), halved)

    def block(owner):
        return acc.at[p2, owner % 2, p1, every, columns(owner)]

    def keep_part(side, value):
        value = value.astype(jnp.float32)[: ROWS - 1]
        span = pl.ds(pl.multiple_of(side * FF_QUARTER, 128), FF_QUARTER)
        gu_ref[:, 0, span] = value[:, :FF_QUARTER]
        gu_ref[:, 1, span] = value[:, FF_QUARTER : 2 * FF_QUARTER]
        down_ref[:, span] = value[:, 2 * FF_QUARTER :]

    far_copy = sender(block(opposite), far, row_device(right))
    from_right_copy = sender(block(left), from_right, row_device(left))
    x_neighbour = row_device((here // 2) * 2 + 1 - x)
    parts_copy = sender(acc.at[p2, 1 - x, p1, every, rest], last, x_neighbour)
    far_copy.wait_recv()
    stage[...] = acc[p2, right % 2, p1, :, columns(right)] + far[...]
    from_left_copy = sender(stage, from_left, row_device(right))
    keep_part(x, acc[p2, x, p1, :, rest])
    parts_copy.wait_recv()
    keep_part(1 - x, last[...])
    from_right_copy.wait_recv()
    from_left_copy.wait_recv()
    total = acc[p2, x, p1, :, columns(here)].astype(jnp.float32)
    total = total + from_left[...].astype(jnp.float32)
    total = total + from_right[...].astype(jnp.float32)
    in_ref[...] = total[: ROWS - 1, :IN_HALF]
    out_ref[...] = total[: ROWS - 1, IN_PAD : IN_PAD + OUT_HALF]
    spare_ref[...] = total[ROWS - 1 :, :128]


def scatter_blocks(arrays, pieces, halved, row_blocks, side, collective_id):
    rows = arrays[0].shape[-2]
    columns = sum(piece[2] for piece in pieces)
    kind = arrays[0].dtype
    block = (rows, columns)
    with_row = row_blocks is not None
    operands = list(arrays)
    in_specs = [pl.BlockSpec(memory_space=pl.ANY)] * len(arrays)
    results = [block]
    last = block
    scratch = []
    if halved:
        last = (rows, columns - 2 * halved)
        results = [
            (rows - 1, IN_HALF),
            (rows - 1, OUT_HALF),
            (rows - 1, 2, FF_HALF),
            (rows - 1, FF_HALF),
            (1, 128),
        ]
        scratch = [pltpu.VMEM((rows, halved), kind)] * 4
    shapes = [jax.ShapeDtypeStruct(shape, jnp.float32) for shape in results]
    if with_row:
        operands.append(row_blocks)
        in_specs.append(pl.BlockSpec(memory_space=pltpu.VMEM))
        shapes.append(jax.ShapeDtypeStruct(row_blocks.shape[1:], jnp.float32))
        scratch = row_scratch(*row_blocks.shape[1:])
    side_work, side_operands, side_shapes = side
    operands += list(side_operands)
    in_specs += [pl.BlockSpec(memory_space=pltpu.VMEM)] * len(side_operands)
    shapes += list(side_shapes)
    side = (side_work, len(side_operands), len(side_shapes))
    return pl.pallas_call(
        lambda *refs: scatter_kernel(pieces, halved, with_row, side, *refs),
        out_shape=tuple(shapes),
        in_specs=in_specs,
        out_specs=(pl.BlockSpec(memory_space=pltpu.VMEM),) * len(shapes),
        scratch_shapes=[
            pltpu.VMEM((4, 2, 4) + block, kind),
            pltpu.VMEM((4, 2, 4) + block, kind),
            pltpu.VMEM((4,) + block, kind),
            pltpu.VMEM((4,) + block, kind),
            pltpu.VMEM((2, 4) + block, kind),
            pltpu.VMEM((2, 4) + block, kind),
            pltpu.VMEM(block, kind),
            pltpu.VMEM(block, kind),
            pltpu.VMEM((2,) + block, kind),
            pltpu.VMEM((2,) + block, kind),
            pltpu.VMEM(last, kind),
            pltpu.SemaphoreType.DMA((4, len(pieces))),
            pltpu.SemaphoreType.DMA((4, len(pieces))),
            pltpu.SemaphoreType.DMA((4, len(pieces))),
            pltpu.SemaphoreType.DMA((16,)),
            pltpu.SemaphoreType.DMA((16,)),
        ]
        + scratch,
        compiler_params=pltpu.CompilerParams(
            collective_id=collective_id, has_side_effects=True, vmem_limit_bytes=VMEM_LIMIT
        ),
    )(*operands)


def weight_grad_work(ins, outs):
    @pl.loop(0, PADDED // 256)
    def _(step):
        span = pl.ds(pl.multiple_of(step * 256, 256), 256)
        outs[0][span, :] = dot(ins[0][:, span], ins[1][...], FIRST).astype(jnp.bfloat16)


def unpad_work(ins, outs):
    for k in range(2):
        outs[k][...] = dot(ins[2][...], ins[k][...], LAST).astype(jnp.bfloat16)


LAST = (((1,), (1,)), ((), ()))
FIRST = (((0,), (0,)), ((), ()))
PLAIN = (((1,), (0,)), ((), ()))


def dot(a, b, dims=PLAIN):
    return lax.dot_general(a, b, dims, preferred_element_type=jnp.float32)


def feed_forward_kernel(
    n_ref,
    c_ref,
    gu_ref,
    down_ref,
    dn_ref,
    part_ref,
    grad_gu_ref,
    grad_down_ref,
    normed,
    partial,
    hidden,
    gate_up_grad,
    far,
    near_left,
    near_right,
    stage,
    send_sem,
    recv_sem,
):
    row_kernel_entry()
    here = row_place()
    left, right, opposite = (here + 3) % 4, (here + 1) % 4, (here + 2) % 4
    to_left, to_right = row_device(left), row_device(right)

    def rows(owner, start=0, size=128):
        return pl.ds(pl.multiple_of(owner * 128 + start, 64), size)

    def copy(number, source, place, device):
        return pltpu.make_async_remote_copy(
            src_ref=source,
            dst_ref=place,
            send_sem=send_sem.at[number],
            recv_sem=recv_sem.at[number],
            device_id=device,
            device_id_type=MESH,
        )

    mine = normed.at[rows(here)]
    low, high = pl.ds(0, 64), pl.ds(64, 64)
    normed_right = copy(0, n_ref, mine, to_right)
    normed_left = copy(1, n_ref, mine, to_left)
    place = normed.at[rows(left, 0, 64)]
    normed_far_low = copy(2, place, place, to_right)
    place = normed.at[rows(right, 64, 64)]
    normed_far_high = copy(3, place, place, to_left)
    far_low = copy(4, partial.at[rows(opposite, 0, 64)], far.at[0], to_right)
    far_high = copy(5, partial.at[rows(opposite, 64, 64)], far.at[1], to_left)
    near_low = copy(6, partial.at[rows(left, 0, 64)], near_right.at[low], to_left)
    near_high = copy(7, partial.at[rows(right, 64, 64)], near_left.at[high], to_right)
    sum_low = copy(8, stage.at[0], near_left.at[low], to_right)
    sum_high = copy(9, stage.at[1], near_right.at[high], to_left)
    normed_right.start()
    normed_left.start()
    normed[rows(here), :] = n_ref[...]

    @pl.loop(0, 4)
    def _(step):
        turn = jnp.where(step == 1, 3, jnp.where(step == 2, 1, jnp.where(step == 3, 2, 0)))
        owner = (here + turn) % 4

        @pl.when(step == 1)
        def _():
            normed_right.wait_recv()
            normed_far_low.start()

        @pl.when(step == 2)
        def _():
            normed_left.wait_recv()
            normed_far_high.start()

        @pl.when(step == 3)
        def _():
            normed_far_low.wait_recv()
            normed_far_high.wait_recv()

        gate_vals = dot(normed[rows(owner), :], gu_ref[...])
        hidden_grad = dot(c_ref[rows(owner), :], down_ref[...])
        gate = gate_vals[:, :FF_QUARTER]
        upper = gate_vals[:, FF_QUARTER:]
        sigma = jax.nn.sigmoid(gate)
        silu_vals = gate * sigma
        hidden[rows(owner), :] = (silu_vals * upper).astype(jnp.bfloat16)
        gate_grad = hidden_grad * upper * sigma * (1.0 + gate * (1.0 - sigma))
        upper_grad = hidden_grad * silu_vals
        both = jnp.concatenate([gate_grad, upper_grad], axis=1).astype(jnp.bfloat16)
        gate_up_grad[rows(owner), :] = both
        partial[rows(owner), :] = dot(both, gu_ref[...], LAST).astype(jnp.bfloat16)

        @pl.when(step == 1)
        def _():
            near_low.start()

        @pl.when(step == 2)
        def _():
            near_high.start()

        @pl.when(step == 3)
        def _():
            far_low.start()
            far_high.start()

    @pl.loop(0, 4)
    def _(owner):
        part_ref[rows(owner), :] = dot(hidden[rows(owner), :], down_ref[...], LAST).astype(
            jnp.bfloat16
        )

    far_low.wait_recv()
    stage[0] = partial[rows(right, 0, 64), :] + far[0]
    sum_low.start()
    far_high.wait_recv()
    stage[1] = partial[rows(left, 64, 64), :] + far[1]
    sum_high.start()

    @pl.loop(0, PADDED // 256)
    def _(step):
        span = pl.ds(pl.multiple_of(step * 256, 256), 256)
        grad_gu_ref[span, :] = dot(normed[:, span], gate_up_grad[...], FIRST).astype(jnp.bfloat16)
        grad_down_ref[span, :] = dot(c_ref[:, span], hidden[...], FIRST).astype(jnp.bfloat16)

    for arrived in (near_low, near_high, sum_low, sum_high):
        arrived.wait_recv()
    total = partial[rows(here), :].astype(jnp.float32) + near_left[...].astype(jnp.float32)
    dn_ref[...] = total + near_right[...].astype(jnp.float32)
    for sent in (normed_right, normed_left, normed_far_low, normed_far_high, far_low, far_high):
        sent.wait_send()
    for sent in (near_low, near_high, sum_low, sum_high):
        sent.wait_send()


def feed_forward(normed, cotangent, weight_gu, weight_down, collective_id):
    kind = jnp.bfloat16
    return pl.pallas_call(
        feed_forward_kernel,
        out_shape=(
            jax.ShapeDtypeStruct((128, PADDED), jnp.float32),
            jax.ShapeDtypeStruct((512, PADDED), kind),
            jax.ShapeDtypeStruct(weight_gu.shape, kind),
            jax.ShapeDtypeStruct(weight_down.shape, kind),
        ),
        in_specs=[pl.BlockSpec(memory_space=pltpu.VMEM)] * 4,
        out_specs=(pl.BlockSpec(memory_space=pltpu.VMEM),) * 4,
        scratch_shapes=[
            pltpu.VMEM((512, PADDED), kind),
            pltpu.VMEM((512, PADDED), kind),
            pltpu.VMEM((512, FF_QUARTER), kind),
            pltpu.VMEM((512, 2 * FF_QUARTER), kind),
            pltpu.VMEM((2, 64, PADDED), kind),
            pltpu.VMEM((128, PADDED), kind),
            pltpu.VMEM((128, PADDED), kind),
            pltpu.VMEM((2, 64, PADDED), kind),
            pltpu.SemaphoreType.DMA((10,)),
            pltpu.SemaphoreType.DMA((10,)),
        ],
        compiler_params=pltpu.CompilerParams(
            collective_id=collective_id, has_side_effects=True, vmem_limit_bytes=VMEM_LIMIT
        ),
        cost_estimate=pl.CostEstimate(
            flops=7 * 10**9, bytes_accessed=10**7, transcendentals=4 * 10**5
        ),
    )(normed, cotangent, weight_gu, weight_down)


def load_tiles(table_ref, kv_hbm, kv, sems, tiles):
    @pl.loop(0, tiles)
    def _(tile):
        for j in range(8):
            block = tile * 8 + j
            pltpu.make_async_copy(
                kv_hbm.at[table_ref[block]],
                kv.at[pl.ds(pl.multiple_of(block * 64, 64), 64)],
                sems.at[tile],
            ).start()


def wait_tile(kv, sems, tile):
    part = kv.at[pl.ds(pl.multiple_of(tile * TILE, TILE), TILE)]
    pltpu.make_async_copy(part, part, sems.at[tile]).wait()


def visible_keys(tile, pair, first_row, rows):
    shape = (rows, TILE)
    row = first_row + lax.broadcasted_iota(jnp.int32, shape, 0)
    key = tile * TILE + lax.broadcasted_iota(jnp.int32, shape, 1)
    order = jnp.where(row < QROWS // 2, pair, 127 - pair) * 64 + row % 64
    return key <= order


def head_parts():
    for g in range(KEY_VALUE_HEADS):
        for half in range(2):
            for h in range(GROUP):
                rows = slice((half * GROUP + h) * 64, (half * GROUP + h) * 64 + 64)
                column = (GROUP * g + h) * HEAD_SIZE
                yield g, rows, slice(half * 64, half * 64 + 64), slice(column, column + 64)


def run_tiles(pair, step):
    low_tiles = (pair + 8) // 8
    high_tiles = (135 - pair) // 8

    @pl.loop(0, low_tiles - 1)
    def _(tile):
        step(tile, 0, QROWS, False)

    step(low_tiles - 1, 0, QROWS, True)

    @pl.loop(low_tiles, high_tiles - 1)
    def _(tile):
        step(tile, QROWS // 2, QROWS // 2, False)

    step(high_tiles - 1, QROWS // 2, QROWS // 2, True)


def lane_parts(value):
    return [value[:, k * 128 : k * 128 + 128] for k in range(TILE // 128)]


def attend_kernel(table_ref, pair_ref, q_ref, kv_hbm, out_ref, top_ref, sum_ref, kv, q, acc, sems):
    pair = pair_ref[0]
    high_tiles = (135 - pair) // 8
    load_tiles(table_ref, kv_hbm, kv, sems, high_tiles)
    q[...] = jnp.zeros(q.shape, q.dtype)
    for g, rows, tokens, columns in head_parts():
        q[g, rows, 0:64] = q_ref[tokens, columns]
    acc[...] = jnp.zeros(acc.shape, jnp.float32)
    top_ref[...] = jnp.full(top_ref.shape, -1e30, jnp.float32)
    sum_ref[...] = jnp.zeros(sum_ref.shape, jnp.float32)

    def step(tile, first_row, rows, masked):
        wait_tile(kv, sems, tile)
        span = slice(first_row, first_row + rows)
        if masked:
            seen = visible_keys(tile, pair, first_row, rows)
        heads = range(KEY_VALUE_HEADS)
        keys = [
            kv[pl.ds(pl.multiple_of(tile * TILE, TILE), TILE), g * 128 : g * 128 + 128]
            for g in heads
        ]
        scores = [dot(q[g, span, :], keys[g], LAST) for g in heads]
        if masked:
            scores = [jnp.where(seen, score, -1e30) for score in scores]
        parts = [lane_parts(score) for score in scores]
        best = [
            jnp.maximum(jnp.maximum(p[0], p[1]), jnp.maximum(p[2], p[3])) for p in parts
        ]
        before = [top_ref[g, span, :] for g in heads]
        highest = [
            jnp.maximum(before[g], jnp.max(best[g], axis=1, keepdims=True)) for g in heads
        ]
        shrink = [jnp.exp(before[g] - highest[g]) for g in heads]
        parts = [[jnp.exp(part - highest[g]) for part in parts[g]] for g in heads]
        for g in heads:
            p = parts[g]
            top_ref[g, span, :] = highest[g]
            sum_ref[g, span, :] = sum_ref[g, span, :] * shrink[g] + ((p[0] + p[1]) + (p[2] + p[3]))
        mixed = [
            dot(jnp.concatenate([p.astype(jnp.bfloat16) for p in parts[g]], axis=1), keys[g])
            for g in heads
        ]
        for g in heads:
            acc[g, span, :] = acc[g, span, :] * shrink[g] + mixed[g]

    run_tiles(pair, step)
    for g in range(KEY_VALUE_HEADS):
        total = jnp.sum(sum_ref[g], axis=1, keepdims=True)
        sum_ref[g] = jnp.broadcast_to(total, sum_ref.shape[1:])
        acc[g] = acc[g] / sum_ref[g]
    for g, rows, tokens, columns in head_parts():
        out_ref[tokens, columns] = acc[g, rows, 64:128]


def attend(table, pair, q, kv):
    heads = (KEY_VALUE_HEADS, QROWS, 128)
    return pl.pallas_call(
        attend_kernel,
        out_shape=(
            jax.ShapeDtypeStruct((128, WIDTH), jnp.float32),
            jax.ShapeDtypeStruct(heads, jnp.float32),
            jax.ShapeDtypeStruct(heads, jnp.float32),
        ),
        in_specs=[
            pl.BlockSpec(memory_space=pltpu.SMEM),
            pl.BlockSpec(memory_space=pltpu.SMEM),
            pl.BlockSpec(memory_space=pltpu.VMEM),
            pl.BlockSpec(memory_space=pl.ANY),
        ],
        out_specs=(pl.BlockSpec(memory_space=pltpu.VMEM),) * 3,
        scratch_shapes=[
            pltpu.VMEM((8192, 640), jnp.bfloat16),
            pltpu.VMEM(heads, jnp.bfloat16),
            pltpu.VMEM(heads, jnp.float32),
            pltpu.SemaphoreType.DMA((16,)),
        ],
        compiler_params=pltpu.CompilerParams(vmem_limit_bytes=VMEM_LIMIT),
        cost_estimate=pl.CostEstimate(
            flops=4 * 10**9, bytes_accessed=10**7, transcendentals=8 * 10**6
        ),
    )(table, pair, q, kv)


def attend_back_kernel(
    table_ref,
    pair_ref,
    q_ref,
    grad_ref,
    out_ref,
    top_ref,
    sum_ref,
    kv_hbm,
    dq_ref,
    dkv_hbm,
    kv,
    dkv,
    q,
    gs,
    q_turned,
    g_turned,
    shift,
    acc,
    sems,
    out_sems,
):
    pair = pair_ref[0]
    high_tiles = (135 - pair) // 8
    load_tiles(table_ref, kv_hbm, kv, sems, high_tiles)

    def store(tile):
        for j in range(8):
            block = tile * 8 + j
            pltpu.make_async_copy(
                dkv.at[pl.ds(pl.multiple_of(block * 64, 64), 64)],
                dkv_hbm.at[table_ref[block]],
                out_sems.at[tile],
            ).start()

    @pl.loop(high_tiles, 16)
    def _(tile):
        dkv[pl.ds(pl.multiple_of(tile * TILE, TILE), TILE), :] = jnp.zeros(
            (TILE, 640), jnp.bfloat16
        )
        store(tile)

    q[...] = jnp.zeros(q.shape, q.dtype)
    gs[...] = jnp.zeros(gs.shape, gs.dtype)
    for g, rows, tokens, columns in head_parts():
        q[g, rows, 0:64] = q_ref[tokens, columns]
        grad = grad_ref[tokens, columns]
        total = sum_ref[g, rows, :]
        gs[g, rows, 64:128] = (grad / total[:, 0:64]).astype(jnp.bfloat16)
        delta = jnp.sum(grad * out_ref[tokens, columns], axis=1, keepdims=True)
        shift[g, rows, :] = delta / total
    for g in range(KEY_VALUE_HEADS):
        q_turned[g] = q[g].T
        g_turned[g] = gs[g].T
    acc[...] = jnp.zeros(acc.shape, jnp.float32)

    def step(tile, first_row, rows, masked):
        wait_tile(kv, sems, tile)
        span = slice(first_row, first_row + rows)
        part = pl.ds(pl.multiple_of(tile * TILE, TILE), TILE)
        if masked:
            seen = visible_keys(tile, pair, first_row, rows)
        heads = range(KEY_VALUE_HEADS)
        keys = [kv[part, g * 128 : g * 128 + 128] for g in heads]
        scores = [dot(q[g, span, :], keys[g], LAST) for g in heads]
        prob_grad = [dot(gs[g, span, :], keys[g], LAST) for g in heads]
        if masked:
            scores = [jnp.where(seen, score, -1e30) for score in scores]
        for g in heads:
            top, moved = top_ref[g, span, :], shift[g, span, :]
            probs = [jnp.exp(part_ - top) for part_ in lane_parts(scores[g])]
            grads = [
                (probs[k] * (part_ - moved)).astype(jnp.bfloat16)
                for k, part_ in enumerate(lane_parts(prob_grad[g]))
            ]
            score_grad = jnp.concatenate(grads, axis=1)
            probs_low = jnp.concatenate([prob.astype(jnp.bfloat16) for prob in probs], axis=1)
            both = dot(
                jnp.concatenate([q_turned[g, :, span], g_turned[g, :, span]], axis=1),
                jnp.concatenate([score_grad, probs_low], axis=0),
            )
            acc[g, span, :] = acc[g, span, :] + dot(score_grad, keys[g])
            dkv[part, g * 128 : g * 128 + 128] = both.astype(jnp.bfloat16).T
        store(tile)

    run_tiles(pair, step)
    for g, rows, tokens, columns in head_parts():
        dq_ref[tokens, columns] = acc[g, rows, 0:64]

    @pl.loop(0, 16)
    def _(tile):
        part = dkv.at[pl.ds(pl.multiple_of(tile * TILE, TILE), TILE)]
        pltpu.make_async_copy(part, part, out_sems.at[tile]).wait()


def attend_back(table, pair, q, grad, out, top, total, kv):
    heads = (KEY_VALUE_HEADS, QROWS, 128)
    turned = (KEY_VALUE_HEADS, 128, QROWS)
    return pl.pallas_call(
        attend_back_kernel,
        out_shape=(
            jax.ShapeDtypeStruct((128, WIDTH), jnp.float32),
            jax.ShapeDtypeStruct((128, 64, 640), jnp.bfloat16),
        ),
        in_specs=[pl.BlockSpec(memory_space=pltpu.SMEM)] * 2
        + [pl.BlockSpec(memory_space=pltpu.VMEM)] * 5
        + [pl.BlockSpec(memory_space=pl.ANY)],
        out_specs=(
            pl.BlockSpec(memory_space=pltpu.VMEM),
            pl.BlockSpec(memory_space=pl.ANY),
        ),
        scratch_shapes=[
            pltpu.VMEM((8192, 640), jnp.bfloat16),
            pltpu.VMEM((8192, 640), jnp.bfloat16),
            pltpu.VMEM(heads, jnp.bfloat16),
            pltpu.VMEM(heads, jnp.bfloat16),
            pltpu.VMEM(turned, jnp.bfloat16),
            pltpu.VMEM(turned, jnp.bfloat16),
            pltpu.VMEM(heads, jnp.float32),
            pltpu.VMEM(heads, jnp.float32),
            pltpu.SemaphoreType.DMA((16,)),
            pltpu.SemaphoreType.DMA((16,)),
        ],
        compiler_params=pltpu.CompilerParams(vmem_limit_bytes=VMEM_LIMIT),
        cost_estimate=pl.CostEstimate(
            flops=10**10, bytes_accessed=2 * 10**7, transcendentals=8 * 10**6
        ),
    )(table, pair, q, grad, out, top, total, kv)


def pad_columns(value, columns):
    return jnp.pad(value, ((0, 0), (0, columns - value.shape[1])))


def pad_halves(value, half, padded):
    return jnp.concatenate(
        [pad_columns(value[:, :half], padded), pad_columns(value[:, half:], padded)], axis=1
    )


def norm_backward(rows, scale, weighted):
    inner = jnp.sum(weighted * rows, axis=-1, keepdims=True)
    return scale * weighted - rows * scale**3 * inner / WIDTH


def rotate_tiles(values, cosine, sine):
    lane = lax.broadcasted_iota(jnp.int32, (128, 128), 1)
    turned = []
    for k in range(values.shape[1] // 128):
        part = values[:, k * 128 : k * 128 + 128]
        partner = jnp.where(lane % 64 < 32, pltpu.roll(part, 96, 1), pltpu.roll(part, 32, 1))
        turned.append(part * cosine + partner * sine)
    return jnp.concatenate(turned, axis=1)


def project_kernel(
    start_ref, scale_ref, spare_ref, w_ref, cos_ref, sin_ref, n_ref, q_ref, kv_ref, gain_ref
):
    lane = lax.broadcasted_iota(jnp.int32, (ROWS, PADDED), 1)
    row = lax.broadcasted_iota(jnp.int32, (ROWS, PADDED), 0)
    spread = dot(spare_ref[...], jnp.where(lane % ROWS == row, 1.0, 0.0).astype(jnp.bfloat16))
    lane = lax.broadcasted_iota(jnp.int32, (128, PADDED), 1)
    slot = lax.broadcasted_iota(jnp.int32, (128, PADDED), 0)
    spread = jnp.where(lane // ROWS == slot % 64, spread, 0.0)
    gain_first = jnp.sum(spread[:64], axis=0, keepdims=True)
    gain_ref[0:1, :] = gain_first
    gain_ref[1:2, :] = jnp.sum(spread[64:], axis=0, keepdims=True)
    normed = (start_ref[...] * scale_ref[...] * gain_first).astype(jnp.bfloat16)
    n_ref[...] = normed
    projected = dot(normed, w_ref[...])
    natural = jnp.concatenate(
        [projected[:, :IN_HALF], projected[:, IN_PAD : IN_PAD + IN_HALF]], axis=1
    )
    key_width = KEY_VALUE_HEADS * HEAD_SIZE
    turned = rotate_tiles(natural[:, : WIDTH + key_width], cos_ref[...], sin_ref[...])
    q_ref[...] = turned[:, :WIDTH].astype(jnp.bfloat16) * jnp.bfloat16(0.125)
    keys, values = turned[:, WIDTH:], natural[:, WIDTH + key_width :]
    pieces = []
    for g in range(KEY_VALUE_HEADS):
        span = slice(g * HEAD_SIZE, (g + 1) * HEAD_SIZE)
        pieces += [keys[:, span], values[:, span]]
    kv_ref[...] = jnp.concatenate(pieces, axis=1).astype(jnp.bfloat16)


def local_call(kernel, shapes, flops):
    return pl.pallas_call(
        kernel,
        out_shape=tuple(jax.ShapeDtypeStruct(shape, kind) for shape, kind in shapes),
        compiler_params=pltpu.CompilerParams(vmem_limit_bytes=VMEM_LIMIT),
        cost_estimate=pl.CostEstimate(flops=flops, bytes_accessed=6 * 10**6, transcendentals=0),
    )


def project(start, scale, spare, weight, cosine, sine):
    low, full = jnp.bfloat16, jnp.float32
    shapes = (
        ((128, PADDED), low),
        ((128, WIDTH), low),
        ((128, 2 * KEY_VALUE_HEADS * HEAD_SIZE), low),
        ((2, PADDED), full),
    )
    return local_call(project_kernel, shapes, 5 * 10**8)(start, scale, spare, weight, cosine, sine)


def project_back_kernel(
    dq_ref,
    kv_ref,
    start_ref,
    scale_ref,
    gain_ref,
    gain_two_ref,
    resid_ref,
    n_ref,
    w_ref,
    cos_ref,
    sin_ref,
    grad_ref,
    input_ref,
):
    key_width = KEY_VALUE_HEADS * HEAD_SIZE
    kv = kv_ref[...]
    keys = [kv[:, g * 128 : g * 128 + 64] for g in range(KEY_VALUE_HEADS)]
    values = [kv[:, g * 128 + 64 : g * 128 + 128] for g in range(KEY_VALUE_HEADS)]
    turned = rotate_tiles(
        jnp.concatenate([dq_ref[...] * 0.125] + keys, axis=1), cos_ref[...], -sin_ref[...]
    )
    natural = jnp.concatenate([turned] + values, axis=1).astype(jnp.bfloat16)
    blank = jnp.zeros((128, IN_PAD - IN_HALF), jnp.bfloat16)
    grads = jnp.concatenate([natural[:, :IN_HALF], blank, natural[:, IN_HALF:], blank], axis=1)
    back = dot(grads, w_ref[...], LAST)
    start, scale = start_ref[...], scale_ref[...]
    gain_grad = jnp.sum(back * start * scale, axis=0, keepdims=True)
    through = norm_backward(start, scale, back * gain_ref[0:1, :])
    input_ref[...] = (resid_ref[...] + through).astype(jnp.bfloat16)
    for k in range(PADDED // 256):
        span = slice(k * 256, k * 256 + 256)
        grad_ref[span, :] = dot(n_ref[:, span], grads, FIRST).astype(jnp.bfloat16)
    slot = lax.broadcasted_iota(jnp.int32, (64, PADDED), 0)
    lane = lax.broadcasted_iota(jnp.int32, (64, PADDED), 1)
    picks = jnp.where((lane // ROWS == slot) & (lane % ROWS < ROWS - 1), 1.0, 0.0)
    row = lax.broadcasted_iota(jnp.int32, (PADDED, 128), 0)
    column = lax.broadcasted_iota(jnp.int32, (PADDED, 128), 1)
    fold = jnp.where(row % ROWS == column, 1.0, 0.0).astype(jnp.bfloat16)
    row = lax.broadcasted_iota(jnp.int32, (PADDED, 64), 0)
    column = lax.broadcasted_iota(jnp.int32, (PADDED, 64), 1)
    place = jnp.where(row == column * ROWS + ROWS - 1, 1.0, 0.0).astype(jnp.bfloat16)
    for start_column, gain in ((0, gain_grad), (IN_PAD, gain_two_ref[...])):
        by_slot = dot((picks * gain).astype(jnp.bfloat16), fold).astype(jnp.bfloat16)
        span = slice(start_column, start_column + 128)
        grad_ref[:, span] = grad_ref[:, span] + dot(place, by_slot).astype(jnp.bfloat16)


def project_back(*operands):
    shapes = (((PADDED, IN_COLS), jnp.bfloat16), ((128, PADDED), jnp.bfloat16))
    return local_call(project_back_kernel, shapes, 10**9)(*operands)


def on_device(
    inputs,
    cotangent,
    positions,
    pair_index,
    input_projection,
    project_out,
    gate_up,
    down_weight,
    norm_gains,
):
    half = lax.axis_index("fsdp")
    pair = pair_index[0, 0]
    key_width = KEY_VALUE_HEADS * HEAD_SIZE
    select = (
        lax.broadcasted_iota(jnp.int32, (WIDTH, PADDED), 0) == jnp.asarray(COLUMN_MAP)[None, :]
    ).astype(jnp.bfloat16)

    spare = jnp.pad(norm_gains.T, ((0, 0), (0, 1)))
    own_in = pad_columns(
        jnp.concatenate([input_projection, pad_columns(spare, IN_HALF)], axis=0), IN_PAD
    )
    own_in = own_in.at[15, ROWS].set(pair.astype(jnp.bfloat16))
    own_out = jnp.pad(project_out, ((0, 1), (0, OUT_PAD - OUT_HALF)))
    gate_up_parts = gate_up.reshape(15, 2, 2, FF_QUARTER).transpose(2, 0, 1, 3)
    gate_up_parts = gate_up_parts.reshape(2, 15, 2 * FF_QUARTER)
    down_parts = down_weight.reshape(15, 2, FF_QUARTER).transpose(1, 0, 2)
    spare_row = ((0, 0), (0, 1), (0, 0))
    upstream = dot(cotangent[0], select)
    weight_in, weight_out, weight_gu, weight_down, row_cotangent = gather_blocks(
        (
            own_in,
            own_out,
            jnp.pad(gate_up_parts, spare_row),
            jnp.pad(down_parts, spare_row),
        ),
        ("row", "row", "split", "split"),
        upstream.astype(jnp.bfloat16),
        0,
    )
    weight_in = weight_in.reshape(PADDED, IN_COLS)
    weight_out = weight_out.reshape(PADDED, 2 * OUT_PAD)
    weight_gu = weight_gu.reshape(PADDED, 2 * FF_QUARTER)
    weight_down = weight_down.reshape(PADDED, FF_QUARTER)
    row_cotangent = row_cotangent.reshape(512, PADDED)
    blocks_in = weight_in.reshape(64, ROWS, IN_COLS)
    spare_first = blocks_in[:, 15, : 2 * ROWS]
    spare_second = blocks_in[:, 15, IN_PAD : IN_PAD + 2 * ROWS]
    held = jnp.arange(PADDED) % ROWS < 15
    labels = jnp.where(half == 0, spare_first, spare_second)[:, ROWS].astype(jnp.int32)
    slots = jnp.arange(64, dtype=jnp.int32)
    blocks = jnp.stack([labels, 127 - labels], axis=1).reshape(128)
    places = jnp.stack([2 * slots, 2 * slots + 1], axis=1).reshape(128)
    hits = blocks[None, :] == jnp.arange(128, dtype=jnp.int32)[:, None]
    table = jnp.sum(jnp.where(hits, places[None, :], 0), axis=1)

    start = dot(inputs[0], select)
    freqs = jnp.exp(
        -math.log(10000.0) * jnp.arange(HEAD_SIZE // 2, dtype=jnp.float32) * 2.0 / HEAD_SIZE
    )
    angle = positions[0].astype(jnp.float32)[:, None] * freqs[None, :]
    cosine = jnp.tile(jnp.cos(angle), (1, 4))
    sine = jnp.sin(angle)
    sine = jnp.tile(jnp.concatenate([-sine, sine], axis=1), (1, 2))
    scale_one = lax.rsqrt(jnp.sum(start * start, axis=-1, keepdims=True) / WIDTH + EPSILON)
    spare = jnp.concatenate([spare_first[:, :ROWS], spare_second[:, :ROWS]], axis=0)
    normed_low, query_scaled, key_value, gains = project(
        start, scale_one, spare, weight_in, cosine, sine
    )
    gain_second = gains[1]
    all_kv = gather_blocks((key_value,), ("whole",), None, 1)[0].reshape(128, 64, 2 * key_width)
    pair_one = pair.reshape(1)
    attention, top, total = attend(table, pair_one, query_scaled, all_kv)
    mixed_low = pad_halves(attention.astype(jnp.bfloat16), OUT_HALF, OUT_PAD)
    branch = dot(mixed_low, weight_out, LAST)
    resid = start + jnp.where(held, branch, 0.0)
    scale_two = lax.rsqrt(jnp.sum(resid * resid, axis=-1, keepdims=True) / WIDTH + EPSILON)
    normed_two = (resid * scale_two * gain_second).astype(jnp.bfloat16)
    normed_two_grad, ffn_out, grad_gu, grad_down = feed_forward(
        normed_two, row_cotangent, weight_gu, weight_down, 2
    )
    resid_grad = upstream + norm_backward(resid, scale_two, normed_two_grad * gain_second)
    gain_two_grad = jnp.sum(normed_two_grad * resid * scale_two, axis=0, keepdims=True)
    branch_grad_low = resid_grad.astype(jnp.bfloat16)
    mixed_grad = dot(branch_grad_low, weight_out)
    mixed_grad = jnp.concatenate(
        [mixed_grad[:, :OUT_HALF], mixed_grad[:, OUT_PAD : OUT_PAD + OUT_HALF]], axis=1
    )
    query_grad, all_kv_grad = attend_back(
        table, pair_one, query_scaled, mixed_grad, attention, top, total, all_kv
    )
    kv_grad, ffn_out, grad_out = scatter_blocks(
        (all_kv_grad.reshape(2, 4, 4, 2, 128, 2 * key_width),),
        ((0, 0, 2 * key_width, 0),),
        None,
        ffn_out.reshape(4, 128, PADDED),
        (
            weight_grad_work,
            (branch_grad_low, mixed_low),
            (jax.ShapeDtypeStruct((PADDED, 2 * OUT_PAD), jnp.bfloat16),),
        ),
        3,
    )
    layer_out = (resid + ffn_out).astype(jnp.bfloat16)
    grad_in, input_grad = project_back(
        query_grad,
        kv_grad,
        start,
        scale_one,
        gains,
        gain_two_grad,
        resid_grad,
        normed_low,
        weight_in,
        cosine,
        sine,
    )
    own_cols = IN_PAD + OUT_PAD
    narrow = jax.ShapeDtypeStruct((WIDTH, 128), jnp.bfloat16)
    sum_in, sum_out, sum_gu, sum_down, spare, layer_out, input_grad = scatter_blocks(
        tuple(
            grad.reshape(2, 4, 4, 2, ROWS, grad.shape[1])
            for grad in (grad_in, grad_out, grad_gu, grad_down)
        ),
        (
            (0, 0, IN_PAD, 0),
            (0, IN_PAD, IN_PAD, own_cols),
            (1, 0, OUT_PAD, IN_PAD),
            (1, OUT_PAD, OUT_PAD, own_cols + IN_PAD),
            (2, 0, 2 * FF_QUARTER, 2 * own_cols),
            (3, 0, FF_QUARTER, 2 * own_cols + 2 * FF_QUARTER),
        ),
        own_cols,
        None,
        (unpad_work, (layer_out, input_grad, select), (narrow, narrow)),
        4,
    )
    return (
        layer_out.T[None],
        input_grad.T[None],
        sum_in,
        sum_out,
        sum_gu,
        sum_down,
        spare[0, :15].reshape(15, 1),
    )


def solution(mesh):
    in_specs = (
        P("fsdp", "ctx", None),
        P("fsdp", "ctx", None),
        P("fsdp", "ctx"),
        P("fsdp", "ctx"),
        P("ctx", "fsdp"),
        P("ctx", "fsdp"),
        P("ctx", None, "fsdp"),
        P("ctx", "fsdp"),
        P("ctx", "fsdp"),
    )
    out_specs = (
        P("fsdp", "ctx", None),
        P("fsdp", "ctx", None),
        P("ctx", "fsdp"),
        P("ctx", "fsdp"),
        P("ctx", None, "fsdp"),
        P("ctx", "fsdp"),
        P("ctx", "fsdp"),
    )
    return jax.shard_map(
        on_device, mesh=mesh, in_specs=in_specs, out_specs=out_specs, check_vma=False
    )
```

profile of v0, /device:TPU:0, one launch (start us, length us, event | category | flops | bytes accessed | tf_op | source)
XLA Modules:
  0.0 326.0 jit_solution(11579026270672591722)
XLA Ops:
  2.4 2.3 fusion.25
  4.6 1.1 reshape.188
  7.7 53.6 %shard_map.153 = (bf16[2,4,4,2,16,1792]{5,4,3,2,1,0:T(8,128)(2,1)}, bf16[2,4,4,2,16,1024]{5,4,3,2,1,0:T(8,128)(2,1)}, bf16[2,4,4,2,16,1280]{5,4,3,2,1,0:T(8,128)...) custom-call(bf16[16,896]{1,0:T(8,128)(2,1)} %copy-done.4, bf16[16,512]{1,0:T(8,128)(2,1)} %pad.38.refs_1_, ...), custom_call_target="tpu_custom_call" | custom-call | tf_op jit(solution)/shard_map/pallas_call | solution.py:358
  64.3 1.6 multiply_reduce_fusion.3
  67.4 4.4 %shard_map.154 = (bf16[128,1024]{1,0:T(8,128)(2,1)}, bf16[128,960]{1,0:T(8,128)(2,1)}, bf16[128,640]{1,0:T(8,128)(2,1)}, f32[2,1024]{1,0:T(2,128)}) custom-call(f32[128,1024]{1,0:T(8,128)} %get-tuple-element.97.start_ref, f32[128,1]{1,0:T(8,128)} %copy.60.scale_ref, bf16[128,16]{1,0:T(8,128)(2,1)} %copy.61.spare_ref, bf16[1024,1792]{1,0:T(8,128)(2,1)} %bitcast.61, ...), custom_call_target="tpu_custom_call" | custom-call | flops 500000000 | bytes 6000000 | tf_op jit(solution)/shard_map/pallas_call | solution.py:1155
  71.8 44.0 %shard_map.155 = bf16[2,4,4,2,128,640]{5,4,3,2,1,0:T(8,128)(2,1)} custom-call(bf16[128,640]{1,0:T(8,128)(2,1)} %get-tuple-element.51.refs_0_), custom_call_target="tpu_custom_call" | custom-call | tf_op jit(solution)/shard_map/pallas_call | solution.py:358
  117.0 19.4 %shard_map.156 = (f32[128,960]{1,0:T(8,128)}, f32[5,384,128]{2,1,0:T(8,128)}, f32[5,384,128]{2,1,0:T(8,128)}) custom-call(s32[128]{0:T(128)} %select_reduce_fusion.table_ref, s32[1]{0:T(128)} %bitcast.58.pair_ref, bf16[128,960]{1,0:T(8,128)(2,1)} %get-tuple-element.50.q_ref, bf16[128,64,640]{2,1,0:T(8,128)(2,1)} %bitcast.64), custom_call_target="tpu_custom_call" | custom-call | flops 4000000000 | bytes 10000000 | tf_op jit(solution)/shard_map/pallas_call | solution.py:927
  136.4 1.1 convert_element_type.57
  140.2 34.5 %shard_map.157 = (f32[128,1024]{1,0:T(8,128)}, bf16[512,1024]{1,0:T(8,128)(2,1)}, bf16[1024,1280]{1,0:T(8,128)(2,1)}, bf16[1024,640]{1,0:T(8,128)(2,1)}) custom-call(bf16[128,1024]{1,0:T(8,128)(2,1)} %multiply_convert_fusion.n_ref, bf16[512,1024]{1,0:T(8,128)(2,1)} %bitcast.90, bf16[1024,1280]{1,0:T(8,128)(2,1)} %bitcast.88, bf16[1024,640]{1,0:T(8,128)(2,1)} %bitcast.89), custom_call_target="tpu_custom_call" | custom-call | flops 7000000000 | bytes 10000000 | tf_op jit(solution)/shard_map/pallas_call | solution.py:785
  174.7 1.8 multiply_reduce_fusion
  176.5 2.1 fusion.21
  180.0 30.1 %shard_map.158 = (f32[128,960]{1,0:T(8,128)}, bf16[128,64,640]{2,1,0:T(8,128)(2,1)}) custom-call(s32[128]{0:T(128)} %select_reduce_fusion.table_ref, s32[1]{0:T(128)} %bitcast.59.pair_ref, bf16[128,960]{1,0:T(8,128)(2,1)} %get-tuple-element.50.q_ref, f32[128,960]{1,0:T(8,128)} %pad_maximum_fusion.grad_ref, f32[128,960]{1,0:T(8,128)} %get-tuple-element.52.out_ref, ...), custom_call_target="tpu_custom_call" | custom-call | flops 10000000000 | bytes 20000000 | tf_op jit(solution)/shard_map/pallas_call | solution.py:1052
  210.1 47.2 %shard_map.159 = (f32[128,640]{1,0:T(8,128)}, f32[128,1024]{1,0:T(8,128)}, bf16[1024,1024]{1,0:T(8,128)(2,1)}) custom-call(bf16[2,4,4,2,128,640]{5,4,3,2,1,0:T(8,128)(2,1)} %bitcast.63, bf16[4,128,1024]{2,1,0:T(8,128)(2,1)} %bitcast.72, bf16[128,1024]{1,0:T(8,128)(2,1)} %copy-done.3, bf16[128,1024]{1,0:T(8,128)(2,1)} %fusion.9.refs_3_), custom_call_target="tpu_custom_call" | custom-call | tf_op jit(solution)/shard_map/pallas_call | solution.py:601
  257.3 1.8 add_convert_fusion.refs_4_
  259.1 7.5 %shard_map.160 = (bf16[1024,1792]{1,0:T(8,128)(2,1)}, bf16[128,1024]{1,0:T(8,128)(2,1)}) custom-call(f32[128,960]{1,0:T(8,128)} %get-tuple-element.61.dq_ref, f32[128,640]{1,0:T(8,128)} %get-tuple-element.64.kv_ref, f32[128,1024]{1,0:T(8,128)} %get-tuple-element.97.start_ref, f32[128,1]{1,0:T(8,128)} %copy.60.scale_ref, ...), custom_call_target="tpu_custom_call" | custom-call | flops 1000000000 | bytes 6000000 | tf_op jit(solution)/shard_map/pallas_call | solution.py:1208
  266.6 2.1 fusion.refs_6_
  268.7 46.9 %shard_map.161 = (f32[15,800]{1,0:T(8,128)}, f32[15,480]{1,0:T(8,128)}, f32[15,2,1280]{2,1,0:T(2,128)}, f32[15,1280]{1,0:T(8,128)}, f32[1,128]{1,0:T(1,128)}, /*...) custom-call(bf16[2,4,4,2,16,1792]{5,4,3,2,1,0:T(8,128)(2,1)} %bitcast.68, bf16[2,4,4,2,16,1024]{5,4,3,2,1,0:T(8,128)(2,1)} %bitcast.70, ...), custom_call_target="tpu_custom_call" | custom-call | tf_op jit(solution)/shard_map/pallas_call | solution.py:601
  315.6 1.1 slice_bitcast_fusion
  316.8 1.7 copy.81
  318.4 1.7 copy.82
  320.1 1.4 copy.83
  321.5 1.4 copy.84
  322.9 1.6 copy.85
  324.5 1.5 copy.86
  (70 shorter events, 12.5 us)
Async XLA Ops:
  0.6 1.7 copy-start
  0.7 63.6 %copy-start.8 = (s32[1024]{0:T(1024)S(1)}, s32[1024]{0:T(1024)}, u32[]{:S(2)}) copy-start(s32[1024]{0:T(1024)} %constant.81.clone) | copy-start | bytes 12292
  0.7 5.7 %copy-start.5 = (bf16[15,1280]{1,0:T(8,128)(2,1)S(1)}, bf16[15,1280]{1,0:T(8,128)(2,1)}, u32[]{:S(2)}) copy-start(bf16[15,1280]{1,0:T(8,128)(2,1)} %param.19) | copy-start | bytes 115204
  0.7 6.4 %copy-start.7 = (bf16[15,480]{1,0:T(8,128)(2,1)S(1)}, bf16[15,480]{1,0:T(8,128)(2,1)}, u32[]{:S(2)}) copy-start(bf16[15,480]{1,0:T(8,128)(2,1)} %param.17) | copy-start | bytes 43204
  0.7 62.7 %copy-start.11 = (s32[1,128]{1,0:T(1,128)S(1)}, s32[1,128]{1,0:T(1,128)}, u32[]{:S(2)}) copy-start(s32[1,128]{1,0:T(1,128)} %param.14) | copy-start | bytes 1540
  0.7 63.6 %copy-start.10 = (bf16[1,128,960]{1,2,0:T(8,128)(2,1)S(1)}, bf16[1,128,960]{1,2,0:T(8,128)(2,1)}, u32[]{:S(2)}) copy-start(bf16[1,128,960]{1,2,0:T(8,128)(2,1)} %param.12) | copy-start | bytes 737284
  2.4 5.3 %copy-start.4 = (bf16[16,896]{1,0:T(8,128)(2,1)}, bf16[16,896]{1,0:T(8,128)(2,1)S(1)}, u32[]{:S(2)}) copy-start(bf16[16,896]{1,0:T(8,128)(2,1)S(1)} %scatter.4.refs_0_) | copy-start | bytes 86020
  117.0 20.6 %copy-start.9 = (pred[512]{0:T(512)(128)(4,1)S(1)}, pred[512]{0:T(512)(128)(4,1)}, u32[]{:S(2)}) copy-start(pred[512]{0:T(512)(128)(4,1)} %constant.80.clone.1) | copy-start | bytes 1540
  117.0 21.4 %copy-start.1 = (bf16[2,4,4,2,16,1024]{5,4,3,2,1,0:T(8,128)(2,1)S(1)}, bf16[2,4,4,2,16,1024]{5,4,3,2,1,0:T(8,128)(2,1)}, u32[]{:S(2)}) copy-start(bf16[2,4,4,2,16,1024]{5,4,3,2,1,0:T(8,128)(2,1)} %get-tuple-element.53) | copy-start | bytes 6291460
  117.0 21.4 %copy-start.2 = (f32[128,1024]{1,0:T(8,128)S(1)}, f32[128,1024]{1,0:T(8,128)}, u32[]{:S(2)}) copy-start(f32[128,1024]{1,0:T(8,128)} %get-tuple-element.97.start_ref) | copy-start | bytes 1572868
  136.4 2.9 copy-start.6
  178.6 31.6 %copy-start.3 = (bf16[128,1024]{1,0:T(8,128)(2,1)}, bf16[128,1024]{1,0:T(8,128)(2,1)S(1)}, u32[]{:S(2)}) copy-start(bf16[128,1024]{1,0:T(8,128)(2,1)S(1)} %get-tuple-element.81.refs_2_) | copy-start | bytes 786436
where the time goes:
time: 327 us; the launch traced here: 326 us
  Pallas kernels  288 us (88%)
  local copies, waits for them, and re-layouts  18.3 us (6%)
  other arithmetic  13.1 us (4%)
  matrix products  5.26 us (2%)
    pallas_call x2, Pallas kernels, gather_blocks(): pl.pallas_call(lambda *refs: gather_kernel(modes, int(with_row), *refs),...  97.6 us
    pallas_call x2, Pallas kernels, scatter_blocks(): pl.pallas_call(lambda *refs: scatter_kernel(pieces, halved, with_row, sid...  94.1 us
    pallas_call x1, Pallas kernels, feed_forward(): pl.pallas_call(feed_forward_kernel, out_shape=(jax.ShapeDtypeStruct((128,...  34.5 us
    pallas_call x1, Pallas kernels, attend_back(): pl.pallas_call(attend_back_kernel, out_shape=(jax.ShapeDtypeStruct((128,...  30.1 us
    pallas_call x1, Pallas kernels, attend(): pl.pallas_call(attend_kernel, out_shape=(jax.ShapeDtypeStruct((128, WIDTH...  19.4 us
    unnamed x32, local copies, waits for them, and re-layouts  9.46 us
    pallas_call x1, Pallas kernels, project_back(): return local_call(project_back_kernel, shapes, 10 ** 9)(*operands)  7.5 us

commit v1 on v0

--- a/solution.py
+++ b/solution.py
@@ -233,7 +233,10 @@
 
         @pl.when(core == chosen)
         def _(chosen=chosen):
-            gather_body(chosen, modes, with_row, ins, outs, *refs)
+            if modes == ("whole",):
+                gather_fine(chosen, ins[0], outs[0], *refs[:3])
+            else:
+                gather_body(chosen, modes, with_row, ins, outs, *refs)
 
 
 def gather_body(
@@ -341,6 +344,88 @@
         row_sender.finish()
 
 
+def gather_fine(core, in_ref, out_ref, local_sem, send_sem, recv_sem):
+    x, p1, p2, _ = coordinates()
+    across, right1, left1, right2, left2, sibling = neighbours(x, p1, p2, core)
+    p1p, p1m, p1o = (p1 + 1) % 4, (p1 + 3) % 4, (p1 + 2) % 4
+    p2p, p2m, p2o = (p2 + 1) % 4, (p2 + 3) % 4, (p2 + 2) % 4
+    sender = Sender(send_sem, recv_sem)
+
+    def block(side, q1, q2):
+        return block_of(out_ref, core, side, q1, q2)
+
+    def send(place, to, source=None):
+        return sender(place if source is None else source, place, ctx_device(to))
+
+    def near(side, q1, source=None):
+        place = block(side, q1, p2)
+        return send(place, right2, source), send(place, left2, source)
+
+    def cross(side, q2):
+        return send(half_of(out_ref, core, side, q2), sibling)
+
+    def onward_right(copies, q1):
+        copies[0].wait_recv()
+        return send(block(x, q1, p2m), right2)
+
+    def onward_left(copies, q1):
+        copies[1].wait_recv()
+        return send(block(1 - x, q1, p2p), left2)
+
+    mine = block(x, p1, p2)
+    local = pltpu.make_async_copy(in_ref, mine, local_sem.at[0])
+    local.start()
+    crossed = send(mine, across, in_ref)
+    own_right = send(mine, right1, in_ref)
+    own_left = send(mine, left1, in_ref)
+    own = near(x, p1, in_ref)
+    own_right.wait_recv()
+    own_far = send(block(x, p1m, p2), right1)
+    own_m = near(x, p1m)
+    own_left.wait_recv()
+    own_p = near(x, p1p)
+    crossed.wait_recv()
+    there = block(1 - x, p1, p2)
+    other_left = send(there, left1)
+    other_right = send(there, right1)
+    other = near(1 - x, p1)
+    far_own = [onward_right(own, p1)]
+    own_far.wait_recv()
+    own_o = near(x, p1o)
+    far_own.append(onward_right(own_m, p1m))
+    far_own.append(onward_right(own_p, p1p))
+    local.wait()
+    last = [cross(x, p2)]
+    other_left.wait_recv()
+    other_far = send(block(1 - x, p1p, p2), left1)
+    other_p = near(1 - x, p1p)
+    other_right.wait_recv()
+    other_m = near(1 - x, p1m)
+    far_other = [onward_left(other, p1)]
+    other_far.wait_recv()
+    other_o = near(1 - x, p1o)
+    last.append(cross(1 - x, p2))
+    far_own.append(onward_right(own_o, p1o))
+    last.append(cross(x, p2m))
+    far_other.append(onward_left(other_p, p1p))
+    far_other.append(onward_left(other_m, p1m))
+    for copies in (own, own_m, own_p, own_o):
+        copies[1].wait_recv()
+    last.append(cross(x, p2p))
+    far_other.append(onward_left(other_o, p1o))
+    last.append(cross(1 - x, p2p))
+    for copies in (other, other_m, other_p, other_o):
+        copies[0].wait_recv()
+    last.append(cross(1 - x, p2m))
+    for side, copies in ((x, far_own), (1 - x, far_other)):
+        for copy in copies:
+            copy.wait_recv()
+        last.append(cross(side, p2o))
+    for copy in last:
+        copy.wait_recv()
+    sender.finish()
+
+
 def gather_blocks(blocks, modes, row_block, collective_id):
     with_row = row_block is not None
     operands = list(blocks)
@@ -354,7 +439,7 @@
     if with_row:
         operands.append(row_block)
         shapes.append(jax.ShapeDtypeStruct((4,) + row_block.shape, row_block.dtype))
-    number = 23 * len(blocks)
+    number = 39 if modes == ("whole",) else 23 * len(blocks)
     return pl.pallas_call(
         lambda *refs: gather_kernel(modes, int(with_row), *refs),
         out_shape=tuple(shapes),

time: 327 us -> 320 us (0.979)
  Pallas kernels: 288 us -> 281 us
    pallas_call x2, Pallas kernels: 97.6 us -> 90.6 us  [gather_blocks(): pl.pallas_call(lambda *refs: gather_kernel(modes, int(with_row), *refs),...]
    pallas_call x2, Pallas kernels: 94.1 us -> 97.7 us  [scatter_blocks(): pl.pallas_call(lambda *refs: scatter_kernel(pieces, halved, with_row, sid...]
where the time goes in v1:
time: 320 us; the launch traced here: 319 us
  Pallas kernels  281 us (88%)
  local copies, waits for them, and re-layouts  18.3 us (6%)
  other arithmetic  13.1 us (4%)
  matrix products  5.26 us (2%)
    pallas_call x2, Pallas kernels, scatter_blocks(): pl.pallas_call(lambda *refs: scatter_kernel(pieces, halved, with_row, sid...  97.7 us
    pallas_call x2, Pallas kernels, gather_blocks(): pl.pallas_call(lambda *refs: gather_kernel(modes, int(with_row), *refs),...  90.6 us
    pallas_call x1, Pallas kernels, feed_forward(): pl.pallas_call(feed_forward_kernel, out_shape=(jax.ShapeDtypeStruct((128,...  33.6 us
    pallas_call x1, Pallas kernels, attend_back(): pl.pallas_call(attend_back_kernel, out_shape=(jax.ShapeDtypeStruct((128,...  28.7 us
    pallas_call x1, Pallas kernels, attend(): pl.pallas_call(attend_kernel, out_shape=(jax.ShapeDtypeStruct((128, WIDTH...  18 us
    unnamed x32, local copies, waits for them, and re-layouts  9.46 us
    pallas_call x1, Pallas kernels, project_back(): return local_call(project_back_kernel, shapes, 10 ** 9)(*operands)  7.5 us

profile of v1, /device:TPU:0, one launch (start us, length us, event | category | flops | bytes accessed | tf_op | source)
XLA Modules:
  0.0 318.9 jit_solution(18256076352395729324)
XLA Ops:
  2.4 2.3 fusion.25
  4.6 1.1 reshape.188
  7.7 53.6 %shard_map.153 = (bf16[2,4,4,2,16,1792]{5,4,3,2,1,0:T(8,128)(2,1)}, bf16[2,4,4,2,16,1024]{5,4,3,2,1,0:T(8,128)(2,1)}, bf16[2,4,4,2,16,1280]{5,4,3,2,1,0:T(8,128)...) custom-call(bf16[16,896]{1,0:T(8,128)(2,1)} %copy-done.4, bf16[16,512]{1,0:T(8,128)(2,1)} %pad.38.refs_1_, ...), custom_call_target="tpu_custom_call" | custom-call | tf_op jit(solution)/shard_map/pallas_call | solution.py:443
  64.3 1.6 multiply_reduce_fusion.3
  67.4 4.4 %shard_map.154 = (bf16[128,1024]{1,0:T(8,128)(2,1)}, bf16[128,960]{1,0:T(8,128)(2,1)}, bf16[128,640]{1,0:T(8,128)(2,1)}, f32[2,1024]{1,0:T(2,128)}) custom-call(f32[128,1024]{1,0:T(8,128)} %get-tuple-element.97.start_ref, f32[128,1]{1,0:T(8,128)} %copy.60.scale_ref, bf16[128,16]{1,0:T(8,128)(2,1)} %copy.61.spare_ref, bf16[1024,1792]{1,0:T(8,128)(2,1)} %bitcast.61, ...), custom_call_target="tpu_custom_call" | custom-call | flops 500000000 | bytes 6000000 | tf_op jit(solution)/shard_map/pallas_call | solution.py:1240
  71.8 37.1 %shard_map.155 = bf16[2,4,4,2,128,640]{5,4,3,2,1,0:T(8,128)(2,1)} custom-call(bf16[128,640]{1,0:T(8,128)(2,1)} %get-tuple-element.51.refs_0_), custom_call_target="tpu_custom_call" | custom-call | tf_op jit(solution)/shard_map/pallas_call | solution.py:443
  110.0 18.0 %shard_map.156 = (f32[128,960]{1,0:T(8,128)}, f32[5,384,128]{2,1,0:T(8,128)}, f32[5,384,128]{2,1,0:T(8,128)}) custom-call(s32[128]{0:T(128)} %select_reduce_fusion.table_ref, s32[1]{0:T(128)} %bitcast.58.pair_ref, bf16[128,960]{1,0:T(8,128)(2,1)} %get-tuple-element.50.q_ref, bf16[128,64,640]{2,1,0:T(8,128)(2,1)} %bitcast.64), custom_call_target="tpu_custom_call" | custom-call | flops 4000000000 | bytes 10000000 | tf_op jit(solution)/shard_map/pallas_call | solution.py:1012
  128.0 1.1 convert_element_type.57
  131.8 33.6 %shard_map.157 = (f32[128,1024]{1,0:T(8,128)}, bf16[512,1024]{1,0:T(8,128)(2,1)}, bf16[1024,1280]{1,0:T(8,128)(2,1)}, bf16[1024,640]{1,0:T(8,128)(2,1)}) custom-call(bf16[128,1024]{1,0:T(8,128)(2,1)} %multiply_convert_fusion.n_ref, bf16[512,1024]{1,0:T(8,128)(2,1)} %bitcast.90, bf16[1024,1280]{1,0:T(8,128)(2,1)} %bitcast.88, bf16[1024,640]{1,0:T(8,128)(2,1)} %bitcast.89), custom_call_target="tpu_custom_call" | custom-call | flops 7000000000 | bytes 10000000 | tf_op jit(solution)/shard_map/pallas_call | solution.py:870
  165.4 1.8 multiply_reduce_fusion
  167.2 2.1 fusion.21
  170.7 28.7 %shard_map.158 = (f32[128,960]{1,0:T(8,128)}, bf16[128,64,640]{2,1,0:T(8,128)(2,1)}) custom-call(s32[128]{0:T(128)} %select_reduce_fusion.table_ref, s32[1]{0:T(128)} %bitcast.59.pair_ref, bf16[128,960]{1,0:T(8,128)(2,1)} %get-tuple-element.50.q_ref, f32[128,960]{1,0:T(8,128)} %pad_maximum_fusion.grad_ref, f32[128,960]{1,0:T(8,128)} %get-tuple-element.52.out_ref, ...), custom_call_target="tpu_custom_call" | custom-call | flops 10000000000 | bytes 20000000 | tf_op jit(solution)/shard_map/pallas_call | solution.py:1137
  199.5 49.6 %shard_map.159 = (f32[128,640]{1,0:T(8,128)}, f32[128,1024]{1,0:T(8,128)}, bf16[1024,1024]{1,0:T(8,128)(2,1)}) custom-call(bf16[2,4,4,2,128,640]{5,4,3,2,1,0:T(8,128)(2,1)} %bitcast.63, bf16[4,128,1024]{2,1,0:T(8,128)(2,1)} %bitcast.72, bf16[128,1024]{1,0:T(8,128)(2,1)} %copy-done.3, bf16[128,1024]{1,0:T(8,128)(2,1)} %fusion.9.refs_3_), custom_call_target="tpu_custom_call" | custom-call | tf_op jit(solution)/shard_map/pallas_call | solution.py:686
  249.1 1.8 add_convert_fusion.refs_4_
  250.9 7.5 %shard_map.160 = (bf16[1024,1792]{1,0:T(8,128)(2,1)}, bf16[128,1024]{1,0:T(8,128)(2,1)}) custom-call(f32[128,960]{1,0:T(8,128)} %get-tuple-element.61.dq_ref, f32[128,640]{1,0:T(8,128)} %get-tuple-element.64.kv_ref, f32[128,1024]{1,0:T(8,128)} %get-tuple-element.97.start_ref, f32[128,1]{1,0:T(8,128)} %copy.60.scale_ref, ...), custom_call_target="tpu_custom_call" | custom-call | flops 1000000000 | bytes 6000000 | tf_op jit(solution)/shard_map/pallas_call | solution.py:1293
  258.4 2.1 fusion.refs_6_
  260.5 48.1 %shard_map.161 = (f32[15,800]{1,0:T(8,128)}, f32[15,480]{1,0:T(8,128)}, f32[15,2,1280]{2,1,0:T(2,128)}, f32[15,1280]{1,0:T(8,128)}, f32[1,128]{1,0:T(1,128)}, /*...) custom-call(bf16[2,4,4,2,16,1792]{5,4,3,2,1,0:T(8,128)(2,1)} %bitcast.68, bf16[2,4,4,2,16,1024]{5,4,3,2,1,0:T(8,128)(2,1)} %bitcast.70, ...), custom_call_target="tpu_custom_call" | custom-call | tf_op jit(solution)/shard_map/pallas_call | solution.py:686
  308.6 1.1 slice_bitcast_fusion
  309.7 1.7 copy.81
  311.4 1.7 copy.82
  313.0 1.4 copy.83
  314.5 1.4 copy.84
  315.8 1.6 copy.85
  317.4 1.5 copy.86
  (70 shorter events, 12.5 us)
Async XLA Ops:
  0.6 1.7 copy-start
  0.7 63.6 %copy-start.8 = (s32[1024]{0:T(1024)S(1)}, s32[1024]{0:T(1024)}, u32[]{:S(2)}) copy-start(s32[1024]{0:T(1024)} %constant.81.clone) | copy-start | bytes 12292
  0.7 5.7 %copy-start.5 = (bf16[15,1280]{1,0:T(8,128)(2,1)S(1)}, bf16[15,1280]{1,0:T(8,128)(2,1)}, u32[]{:S(2)}) copy-start(bf16[15,1280]{1,0:T(8,128)(2,1)} %param.19) | copy-start | bytes 115204
  0.7 6.4 %copy-start.7 = (bf16[15,480]{1,0:T(8,128)(2,1)S(1)}, bf16[15,480]{1,0:T(8,128)(2,1)}, u32[]{:S(2)}) copy-start(bf16[15,480]{1,0:T(8,128)(2,1)} %param.17) | copy-start | bytes 43204
  0.7 62.7 %copy-start.11 = (s32[1,128]{1,0:T(1,128)S(1)}, s32[1,128]{1,0:T(1,128)}, u32[]{:S(2)}) copy-start(s32[1,128]{1,0:T(1,128)} %param.14) | copy-start | bytes 1540
  0.7 63.6 %copy-start.10 = (bf16[1,128,960]{1,2,0:T(8,128)(2,1)S(1)}, bf16[1,128,960]{1,2,0:T(8,128)(2,1)}, u32[]{:S(2)}) copy-start(bf16[1,128,960]{1,2,0:T(8,128)(2,1)} %param.12) | copy-start | bytes 737284
  2.4 5.3 %copy-start.4 = (bf16[16,896]{1,0:T(8,128)(2,1)}, bf16[16,896]{1,0:T(8,128)(2,1)S(1)}, u32[]{:S(2)}) copy-start(bf16[16,896]{1,0:T(8,128)(2,1)S(1)} %scatter.4.refs_0_) | copy-start | bytes 86020
  110.0 19.2 %copy-start.9 = (pred[512]{0:T(512)(128)(4,1)S(1)}, pred[512]{0:T(512)(128)(4,1)}, u32[]{:S(2)}) copy-start(pred[512]{0:T(512)(128)(4,1)} %constant.80.clone.1) | copy-start | bytes 1540
  110.0 19.9 %copy-start.1 = (bf16[2,4,4,2,16,1024]{5,4,3,2,1,0:T(8,128)(2,1)S(1)}, bf16[2,4,4,2,16,1024]{5,4,3,2,1,0:T(8,128)(2,1)}, u32[]{:S(2)}) copy-start(bf16[2,4,4,2,16,1024]{5,4,3,2,1,0:T(8,128)(2,1)} %get-tuple-element.53) | copy-start | bytes 6291460
  110.0 19.9 %copy-start.2 = (f32[128,1024]{1,0:T(8,128)S(1)}, f32[128,1024]{1,0:T(8,128)}, u32[]{:S(2)}) copy-start(f32[128,1024]{1,0:T(8,128)} %get-tuple-element.97.start_ref) | copy-start | bytes 1572868
  128.0 2.9 copy-start.6
  169.3 30.2 %copy-start.3 = (bf16[128,1024]{1,0:T(8,128)(2,1)}, bf16[128,1024]{1,0:T(8,128)(2,1)S(1)}, u32[]{:S(2)}) copy-start(bf16[128,1024]{1,0:T(8,128)(2,1)S(1)} %get-tuple-element.81.refs_2_) | copy-start | bytes 786436

commit v2 on v0

--- a/solution.py
+++ b/solution.py
@@ -214,154 +214,215 @@
     ]
 
 
-class Group:
-    def __init__(self, copies):
-        self.copies = copies
-
-    def wait_recv(self):
-        for copy in self.copies:
-            copy.wait_recv()
-
-
-def gather_kernel(modes, with_row, *refs):
-    count = len(modes)
-    ins, refs = refs[: count + with_row], refs[count + with_row :]
-    outs, refs = refs[: count + with_row], refs[count + with_row :]
-    greet_ctx("row" in modes or with_row)
+def gather_kernel(count, *refs):
+    ins, refs = refs[:count], refs[count:]
+    outs, refs = refs[:count], refs[count:]
+    greet_ctx(count > 1)
     core = coordinates()[3]
     for chosen in range(2):
 
         @pl.when(core == chosen)
         def _(chosen=chosen):
-            gather_body(chosen, modes, with_row, ins, outs, *refs)
-
-
-def gather_body(
-    core, modes, with_row, ins, outs, local_sem, send_sem, recv_sem, row_local, row_send, row_recv
-):
+            gather_body(chosen, ins, outs, *refs)
+
+
+def gather_body(core, ins, outs, local_sem, send_sem, recv_sem, row_local, row_send, row_recv):
     x, p1, p2, _ = coordinates()
-    across, right1, left1, right2, left2, sibling = neighbours(x, p1, p2, core)
-    p1p, p1m = (p1 + 1) % 4, (p1 + 3) % 4
-    p2p, p2m, p2o = (p2 + 1) % 4, (p2 + 3) % 4, (p2 + 2) % 4
+    across = neighbours(x, p1, p2, core)[0]
+    sender = Sender(send_sem, recv_sem)
+    if len(ins) == 1:
+        mine = block_of(outs[0], core, x, p1, p2)
+        local = pltpu.make_async_copy(ins[0], mine, local_sem.at[0])
+        local.start()
+        crossed = sender(ins[0], mine, ctx_device(across))
+        run_all([gather_steps(core, outs[0], sender, x, lambda: None, crossed.wait_recv, ins[0], [local])])
+        sender.finish()
+        return
     place = row_place()
-    row_left, row_right = (place + 3) % 4, (place + 1) % 4
-    sender = Sender(send_sem, recv_sem)
-    arrays = range(len(modes))
-    plain = [k for k in arrays if modes[k] != "row"]
-    rows = [k for k in arrays if modes[k] == "row"]
-    mine = [ins[k].at[x] if modes[k] == "split" else ins[k] for k in arrays]
-    yours = [ins[k].at[1 - x] if modes[k] == "split" else ins[k] for k in arrays]
-
-    def send(places, to, chosen=arrays, sources=None):
-        sources = places if sources is None else sources
-        return Group([sender(sources[k], places[k], ctx_device(to)) for k in chosen])
-
-    def block(side, q1):
-        return [block_of(outs[k], core, side, q1, p2) for k in arrays]
-
-    def half(side, q2):
-        return [half_of(outs[k], core, side, q2) for k in arrays]
-
-    def slot(k, owner):
-        width = ins[k].shape[-1]
+    left, right = (place + 3) % 4, (place + 1) % 4
+    width = ins[0].shape[-1]
+
+    def slot(owner):
         columns = pl.ds(pl.multiple_of((owner // 2) * width, 128), width)
-        return block_of(outs[k], core, owner % 2, p1, p2).at[pl.ds(0, ROWS), columns]
-
-    here = block(x, p1)
-    there = block(1 - x, p1)
+        return block_of(outs[0], core, owner % 2, p1, p2).at[pl.ds(0, ROWS), columns]
+
+    mine = block_of(outs[1], core, x, p1, p2)
     locals_ = [
-        pltpu.make_async_copy(
-            mine[k], slot(k, place) if k in rows else here[k], local_sem.at[k]
-        )
-        for k in arrays
+        pltpu.make_async_copy(ins[0], slot(place), local_sem.at[0]),
+        pltpu.make_async_copy(ins[1].at[x], mine, local_sem.at[1]),
     ]
     for copy in locals_:
         copy.start()
-    row_near = Group(
+    from_left = sender(ins[0], slot(place), row_device(right))
+    from_right = sender(ins[0], slot(place), row_device(left))
+    crossed = sender(ins[1].at[1 - x], mine, ctx_device(across))
+    far = []
+
+    def first_ready():
+        from_left.wait_recv()
+        far.append(sender(slot(left), slot(left), row_device(right)))
+        from_right.wait_recv()
+
+    def second_ready():
+        far[0].wait_recv()
+        locals_[0].wait()
+
+    row_sender = Sender(row_send, row_recv)
+
+    def row_steps():
+        for _ in range(4):
+            yield
+        row = RowGather(ins[2], outs[2], row_local, row_sender)
+        for _ in range(8):
+            yield
+        row.forward()
+        for _ in range(6):
+            yield
+        row.finish()
+
+    run_all(
         [
-            sender(ins[k], slot(k, place), row_device(to))
-            for to in (row_right, row_left)
-            for k in rows
+            gather_steps(
+                core, outs[1], sender, x, lambda: None, crossed.wait_recv, ins[1].at[x], locals_[1:]
+            ),
+            gather_steps(core, outs[0], sender, 1 - x, first_ready, second_ready, None, []),
+            row_steps(),
         ]
     )
-    crossed = send(here, across, plain, yours)
-    own_left = send(here, right1, plain, mine)
-    own_right = send(here, left1, plain, mine)
-    row_near.wait_recv()
-    row_far = Group(
-        [sender(slot(k, row_left), slot(k, row_left), row_device(row_right)) for k in rows]
-    )
-    crossed.wait_recv()
-    other_left = send(there, right1)
-    other_right = send(there, left1)
+    sender.finish()
+    row_sender.finish()
+
+
+def run_all(steps):
+    while steps:
+        going = []
+        for step in steps:
+            try:
+                next(step)
+                going.append(step)
+            except StopIteration:
+                pass
+        steps = going
+
+
+def gather_steps(core, out_ref, sender, first, first_ready, second_ready, source, locals_):
+    x, p1, p2, _ = coordinates()
+    _, right1, left1, right2, left2, sibling = neighbours(x, p1, p2, core)
+    p1p, p1m, p1o = (p1 + 1) % 4, (p1 + 3) % 4, (p1 + 2) % 4
+    p2p, p2m, p2o = (p2 + 1) % 4, (p2 + 3) % 4, (p2 + 2) % 4
+    second = 1 - first
+
+    def block(side, q1, q2):
+        return block_of(out_ref, core, side, q1, q2)
+
+    def send(place, to, origin=None):
+        return sender(place if origin is None else origin, place, ctx_device(to))
+
+    def near(side, q1, origin=None):
+        place = block(side, q1, p2)
+        return send(place, right2, origin), send(place, left2, origin)
+
+    def cross(side, q2):
+        return send(half_of(out_ref, core, side, q2), sibling)
+
+    def onward_right(copies, q1):
+        copies[0].wait_recv()
+        return send(block(first, q1, p2m), right2)
+
+    def onward_left(copies, q1):
+        copies[1].wait_recv()
+        return send(block(second, q1, p2p), left2)
+
+    first_ready()
+    mine = block(first, p1, p2)
+    own_right = send(mine, right1, source)
+    own_left = send(mine, left1, source)
+    own = near(first, p1, source)
+    yield
+    own_right.wait_recv()
+    own_far = send(block(first, p1m, p2), right1)
+    own_m = near(first, p1m)
+    yield
+    own_left.wait_recv()
+    own_p = near(first, p1p)
+    yield
+    second_ready()
+    there = block(second, p1, p2)
+    other_left = send(there, left1)
+    other_right = send(there, right1)
+    other = near(second, p1)
+    yield
+    far_own = [onward_right(own, p1)]
+    yield
+    own_far.wait_recv()
+    own_o = near(first, p1o)
+    yield
+    far_own.append(onward_right(own_m, p1m))
+    yield
+    far_own.append(onward_right(own_p, p1p))
+    yield
     for copy in locals_:
         copy.wait()
-    row_far.wait_recv()
-    own_left.copies += send(here, right1, rows).copies
-    own_right.copies += send(here, left1, rows).copies
-    if with_row:
-        row_sender = Sender(row_send, row_recv)
-        row = RowGather(ins[-1], outs[-1], row_local, row_sender)
-    own_left.wait_recv()
-    own_far = send(block(x, p1m), right1)
-    own_right.wait_recv()
-    own_far.wait_recv()
-    own_left = send(half(x, p2), right2)
-    own_right = send(half(x, p2), left2)
-    last = [send(half(x, p2), sibling)]
+    last = [cross(first, p2)]
+    other_left.wait_recv()
+    other_far = send(block(second, p1p, p2), left1)
+    other_p = near(second, p1p)
+    yield
     other_right.wait_recv()
-    other_far = send(block(1 - x, p1p), left1)
-    other_left.wait_recv()
+    other_m = near(second, p1m)
+    yield
+    far_other = [onward_left(other, p1)]
+    yield
     other_far.wait_recv()
-    other_right = send(half(1 - x, p2), left2)
-    other_left = send(half(1 - x, p2), right2)
-    last.append(send(half(1 - x, p2), sibling))
-    own_left.wait_recv()
-    own_far = send(half(x, p2m), right2)
-    last.append(send(half(x, p2m), sibling))
-    own_right.wait_recv()
-    last.append(send(half(x, p2p), sibling))
-    if with_row:
-        row.forward()
-    other_right.wait_recv()
-    other_far = send(half(1 - x, p2p), left2)
-    last.append(send(half(1 - x, p2p), sibling))
-    other_left.wait_recv()
-    last.append(send(half(1 - x, p2m), sibling))
-    own_far.wait_recv()
-    last.append(send(half(x, p2o), sibling))
-    if with_row:
-        row.finish()
-    other_far.wait_recv()
-    last.append(send(half(1 - x, p2o), sibling))
-    for group in last:
-        group.wait_recv()
-    sender.finish()
-    if with_row:
-        row_sender.finish()
-
-
-def gather_blocks(blocks, modes, row_block, collective_id):
-    with_row = row_block is not None
-    operands = list(blocks)
-    shapes = [
-        jax.ShapeDtypeStruct(
-            (2, 4, 4, 2, block.shape[-2], block.shape[-1] * (2 if mode == "row" else 1)),
-            block.dtype,
-        )
-        for block, mode in zip(blocks, modes)
-    ]
-    if with_row:
-        operands.append(row_block)
-        shapes.append(jax.ShapeDtypeStruct((4,) + row_block.shape, row_block.dtype))
-    number = 23 * len(blocks)
+    other_o = near(second, p1o)
+    last.append(cross(second, p2))
+    yield
+    far_own.append(onward_right(own_o, p1o))
+    last.append(cross(first, p2m))
+    yield
+    far_other.append(onward_left(other_p, p1p))
+    yield
+    far_other.append(onward_left(other_m, p1m))
+    yield
+    for copies in (own, own_m, own_p, own_o):
+        copies[1].wait_recv()
+    last.append(cross(first, p2p))
+    yield
+    far_other.append(onward_left(other_o, p1o))
+    last.append(cross(second, p2p))
+    yield
+    for copies in (other, other_m, other_p, other_o):
+        copies[0].wait_recv()
+    last.append(cross(second, p2m))
+    yield
+    for side, copies in ((first, far_own), (second, far_other)):
+        for copy in copies:
+            copy.wait_recv()
+        last.append(cross(side, p2o))
+        yield
+    for copy in last:
+        copy.wait_recv()
+
+
+def gather_blocks(blocks, collective_id):
+    kind = jnp.bfloat16
+    if len(blocks) == 1:
+        shapes = [(2, 4, 4, 2) + blocks[0].shape]
+    else:
+        att, parts, row = blocks
+        shapes = [
+            (2, 4, 4, 2, att.shape[0], 2 * att.shape[1]),
+            (2, 4, 4, 2) + parts.shape[1:],
+            (4,) + row.shape,
+        ]
+    number = 39 if len(blocks) == 1 else 80
     return pl.pallas_call(
-        lambda *refs: gather_kernel(modes, int(with_row), *refs),
-        out_shape=tuple(shapes),
-        in_specs=[pl.BlockSpec(memory_space=pl.ANY)] * len(operands),
-        out_specs=(pl.BlockSpec(memory_space=pl.ANY),) * len(operands),
+        lambda *refs: gather_kernel(len(blocks), *refs),
+        out_shape=tuple(jax.ShapeDtypeStruct(shape, kind) for shape in shapes),
+        in_specs=[pl.BlockSpec(memory_space=pl.ANY)] * len(blocks),
+        out_specs=(pl.BlockSpec(memory_space=pl.ANY),) * len(blocks),
         scratch_shapes=[
-            pltpu.SemaphoreType.DMA((len(blocks),)),
+            pltpu.SemaphoreType.DMA((2,)),
             pltpu.SemaphoreType.DMA((number,)),
             pltpu.SemaphoreType.DMA((number,)),
             pltpu.SemaphoreType.DMA,
@@ -371,7 +432,7 @@
         compiler_params=pltpu.CompilerParams(
             collective_id=collective_id, has_side_effects=True
         ),
-    )(*operands)
+    )(*blocks)
 
 
 def scatter_kernel(pieces, halved, with_row, side, *refs):
@@ -635,11 +696,6 @@
         outs[0][span, :] = dot(ins[0][:, span], ins[1][...], FIRST).astype(jnp.bfloat16)
 
 
-def unpad_work(ins, outs):
-    for k in range(2):
-        outs[k][...] = dot(ins[2][...], ins[k][...], LAST).astype(jnp.bfloat16)
-
-
 LAST = (((1,), (1,)), ((), ()))
 FIRST = (((0,), (0,)), ((), ()))
 PLAIN = (((1,), (0,)), ((), ()))
@@ -652,8 +708,7 @@
 def feed_forward_kernel(
     n_ref,
     c_ref,
-    gu_ref,
-    down_ref,
+    w_ref,
     dn_ref,
     part_ref,
     grad_gu_ref,
@@ -670,6 +725,8 @@
     recv_sem,
 ):
     row_kernel_entry()
+    gu_ref = w_ref.at[:, pl.ds(0, 2 * FF_QUARTER)]
+    down_ref = w_ref.at[:, pl.ds(2 * FF_QUARTER, FF_QUARTER)]
     here = row_place()
     left, right, opposite = (here + 3) % 4, (here + 1) % 4, (here + 2) % 4
     to_left, to_right = row_device(left), row_device(right)
@@ -780,17 +837,17 @@
         sent.wait_send()
 
 
-def feed_forward(normed, cotangent, weight_gu, weight_down, collective_id):
+def feed_forward(normed, cotangent, weights, collective_id):
     kind = jnp.bfloat16
     return pl.pallas_call(
         feed_forward_kernel,
         out_shape=(
             jax.ShapeDtypeStruct((128, PADDED), jnp.float32),
             jax.ShapeDtypeStruct((512, PADDED), kind),
-            jax.ShapeDtypeStruct(weight_gu.shape, kind),
-            jax.ShapeDtypeStruct(weight_down.shape, kind),
+            jax.ShapeDtypeStruct((PADDED, 2 * FF_QUARTER), kind),
+            jax.ShapeDtypeStruct((PADDED, FF_QUARTER), kind),
         ),
-        in_specs=[pl.BlockSpec(memory_space=pltpu.VMEM)] * 4,
+        in_specs=[pl.BlockSpec(memory_space=pltpu.VMEM)] * 3,
         out_specs=(pl.BlockSpec(memory_space=pltpu.VMEM),) * 4,
         scratch_shapes=[
             pltpu.VMEM((512, PADDED), kind),
@@ -810,7 +867,7 @@
         cost_estimate=pl.CostEstimate(
             flops=7 * 10**9, bytes_accessed=10**7, transcendentals=4 * 10**5
         ),
-    )(normed, cotangent, weight_gu, weight_down)
+    )(normed, cotangent, weights)
 
 
 def load_tiles(table_ref, kv_hbm, kv, sems, tiles):
@@ -868,9 +925,50 @@
     return [value[:, k * 128 : k * 128 + 128] for k in range(TILE // 128)]
 
 
-def attend_kernel(table_ref, pair_ref, q_ref, kv_hbm, out_ref, top_ref, sum_ref, kv, q, acc, sems):
+def load_halves(w_hbm, place, sems, start):
+    width = place.shape[-1]
+    copies = []
+    for k in range(2):
+        columns = pl.ds(k * (IN_PAD + OUT_PAD) + start, width)
+        copies.append(
+            pltpu.make_async_copy(w_hbm.at[pl.ds(0, PADDED), columns], place.at[k], sems.at[k])
+        )
+        copies[-1].start()
+    return copies
+
+
+def held_lanes():
+    return lax.broadcasted_iota(jnp.int32, (128, PADDED), 1) % ROWS < ROWS - 1
+
+
+def norm_scale(values):
+    return lax.rsqrt(jnp.sum(values * values, axis=-1, keepdims=True) / WIDTH + EPSILON)
+
+
+def attend_kernel(
+    table_ref,
+    pair_ref,
+    q_ref,
+    start_ref,
+    gain_ref,
+    kv_hbm,
+    w_hbm,
+    out_ref,
+    top_ref,
+    sum_ref,
+    mixed_ref,
+    resid_ref,
+    normed_ref,
+    kv,
+    q,
+    acc,
+    weight,
+    sems,
+    w_sems,
+):
     pair = pair_ref[0]
     high_tiles = (135 - pair) // 8
+    loads = load_halves(w_hbm, weight, w_sems, IN_PAD)
     load_tiles(table_ref, kv_hbm, kv, sems, high_tiles)
     q[...] = jnp.zeros(q.shape, q.dtype)
     for g, rows, tokens, columns in head_parts():
@@ -920,9 +1018,19 @@
         acc[g] = acc[g] / sum_ref[g]
     for g, rows, tokens, columns in head_parts():
         out_ref[tokens, columns] = acc[g, rows, 64:128]
-
-
-def attend(table, pair, q, kv):
+    mixed_ref[...] = jnp.zeros(mixed_ref.shape, mixed_ref.dtype)
+    mixed_ref[:, :OUT_HALF] = out_ref[:, :OUT_HALF].astype(jnp.bfloat16)
+    mixed_ref[:, OUT_PAD : OUT_PAD + OUT_HALF] = out_ref[:, OUT_HALF:].astype(jnp.bfloat16)
+    for copy in loads:
+        copy.wait()
+    branch = dot(mixed_ref[:, :OUT_PAD], weight[0], LAST)
+    branch = branch + dot(mixed_ref[:, OUT_PAD:], weight[1], LAST)
+    resid = start_ref[...] + jnp.where(held_lanes(), branch, 0.0)
+    resid_ref[...] = resid
+    normed_ref[...] = (resid * norm_scale(resid) * gain_ref[1:2, :]).astype(jnp.bfloat16)
+
+
+def attend(table, pair, q, start, gains, kv, weights):
     heads = (KEY_VALUE_HEADS, QROWS, 128)
     return pl.pallas_call(
         attend_kernel,
@@ -930,38 +1038,50 @@
             jax.ShapeDtypeStruct((128, WIDTH), jnp.float32),
             jax.ShapeDtypeStruct(heads, jnp.float32),
             jax.ShapeDtypeStruct(heads, jnp.float32),
+            jax.ShapeDtypeStruct((128, PADDED), jnp.bfloat16),
+            jax.ShapeDtypeStruct((128, PADDED), jnp.float32),
+            jax.ShapeDtypeStruct((128, PADDED), jnp.bfloat16),
         ),
-        in_specs=[
-            pl.BlockSpec(memory_space=pltpu.SMEM),
-            pl.BlockSpec(memory_space=pltpu.SMEM),
-            pl.BlockSpec(memory_space=pltpu.VMEM),
-            pl.BlockSpec(memory_space=pl.ANY),
-        ],
-        out_specs=(pl.BlockSpec(memory_space=pltpu.VMEM),) * 3,
+        in_specs=[pl.BlockSpec(memory_space=pltpu.SMEM)] * 2
+        + [pl.BlockSpec(memory_space=pltpu.VMEM)] * 3
+        + [pl.BlockSpec(memory_space=pl.ANY)] * 2,
+        out_specs=(pl.BlockSpec(memory_space=pltpu.VMEM),) * 6,
         scratch_shapes=[
             pltpu.VMEM((8192, 640), jnp.bfloat16),
             pltpu.VMEM(heads, jnp.bfloat16),
             pltpu.VMEM(heads, jnp.float32),
+            pltpu.VMEM((2, PADDED, OUT_PAD), jnp.bfloat16),
             pltpu.SemaphoreType.DMA((16,)),
+            pltpu.SemaphoreType.DMA((2,)),
         ],
         compiler_params=pltpu.CompilerParams(vmem_limit_bytes=VMEM_LIMIT),
         cost_estimate=pl.CostEstimate(
             flops=4 * 10**9, bytes_accessed=10**7, transcendentals=8 * 10**6
         ),
-    )(table, pair, q, kv)
+    )(table, pair, q, start, gains, kv, weights)
 
 
 def attend_back_kernel(
     table_ref,
     pair_ref,
     q_ref,
-    grad_ref,
+    normed_grad_ref,
+    resid_ref,
+    upstream_ref,
+    gain_ref,
     out_ref,
     top_ref,
     sum_ref,
     kv_hbm,
+    w_hbm,
     dq_ref,
     dkv_hbm,
+    resid_grad_ref,
+    branch_grad_ref,
+    gain_grad_ref,
+    grad_ref,
+    weight,
+    w_sems,
     kv,
     dkv,
     q,
@@ -975,6 +1095,7 @@
 ):
     pair = pair_ref[0]
     high_tiles = (135 - pair) // 8
+    loads = load_halves(w_hbm, weight, w_sems, IN_PAD)
     load_tiles(table_ref, kv_hbm, kv, sems, high_tiles)
 
     def store(tile):
@@ -993,6 +1114,18 @@
         )
         store(tile)
 
+    resid, normed_grad = resid_ref[...], normed_grad_ref[...]
+    scale = norm_scale(resid)
+    gain_grad_ref[...] = jnp.sum(normed_grad * resid * scale, axis=0, keepdims=True)
+    resid_grad = upstream_ref[...] + norm_backward(resid, scale, normed_grad * gain_ref[1:2, :])
+    resid_grad_ref[...] = resid_grad
+    branch_grad = resid_grad.astype(jnp.bfloat16)
+    branch_grad_ref[...] = branch_grad
+    for copy in loads:
+        copy.wait()
+    for k in range(2):
+        mixed_grad = dot(branch_grad, weight[k])
+        grad_ref[:, k * OUT_HALF : (k + 1) * OUT_HALF] = mixed_grad[:, :OUT_HALF]
     q[...] = jnp.zeros(q.shape, q.dtype)
     gs[...] = jnp.zeros(gs.shape, gs.dtype)
     for g, rows, tokens, columns in head_parts():
@@ -1046,7 +1179,7 @@
         pltpu.make_async_copy(part, part, out_sems.at[tile]).wait()
 
 
-def attend_back(table, pair, q, grad, out, top, total, kv):
+def attend_back(table, pair, q, normed_grad, resid, upstream, gains, out, top, total, kv, weights):
     heads = (KEY_VALUE_HEADS, QROWS, 128)
     turned = (KEY_VALUE_HEADS, 128, QROWS)
     return pl.pallas_call(
@@ -1054,15 +1187,22 @@
         out_shape=(
             jax.ShapeDtypeStruct((128, WIDTH), jnp.float32),
             jax.ShapeDtypeStruct((128, 64, 640), jnp.bfloat16),
+            jax.ShapeDtypeStruct((128, PADDED), jnp.float32),
+            jax.ShapeDtypeStruct((128, PADDED), jnp.bfloat16),
+            jax.ShapeDtypeStruct((1, PADDED), jnp.float32),
         ),
         in_specs=[pl.BlockSpec(memory_space=pltpu.SMEM)] * 2
-        + [pl.BlockSpec(memory_space=pltpu.VMEM)] * 5
-        + [pl.BlockSpec(memory_space=pl.ANY)],
+        + [pl.BlockSpec(memory_space=pltpu.VMEM)] * 8
+        + [pl.BlockSpec(memory_space=pl.ANY)] * 2,
         out_specs=(
             pl.BlockSpec(memory_space=pltpu.VMEM),
             pl.BlockSpec(memory_space=pl.ANY),
-        ),
+        )
+        + (pl.BlockSpec(memory_space=pltpu.VMEM),) * 3,
         scratch_shapes=[
+            pltpu.VMEM((128, WIDTH), jnp.float32),
+            pltpu.VMEM((2, PADDED, OUT_PAD), jnp.bfloat16),
+            pltpu.SemaphoreType.DMA((2,)),
             pltpu.VMEM((8192, 640), jnp.bfloat16),
             pltpu.VMEM((8192, 640), jnp.bfloat16),
             pltpu.VMEM(heads, jnp.bfloat16),
@@ -1078,7 +1218,7 @@
         cost_estimate=pl.CostEstimate(
             flops=10**10, bytes_accessed=2 * 10**7, transcendentals=8 * 10**6
         ),
-    )(table, pair, q, grad, out, top, total, kv)
+    )(table, pair, q, normed_grad, resid, upstream, gains, out, top, total, kv, weights)
 
 
 def pad_columns(value, columns):
@@ -1107,8 +1247,19 @@
 
 
 def project_kernel(
-    start_ref, scale_ref, spare_ref, w_ref, cos_ref, sin_ref, n_ref, q_ref, kv_ref, gain_ref
+    start_ref,
+    spare_ref,
+    cos_ref,
+    sin_ref,
+    w_hbm,
+    n_ref,
+    q_ref,
+    kv_ref,
+    gain_ref,
+    weight,
+    w_sems,
 ):
+    loads = load_halves(w_hbm, weight, w_sems, 0)
     lane = lax.broadcasted_iota(jnp.int32, (ROWS, PADDED), 1)
     row = lax.broadcasted_iota(jnp.int32, (ROWS, PADDED), 0)
     spread = dot(spare_ref[...], jnp.where(lane % ROWS == row, 1.0, 0.0).astype(jnp.bfloat16))
@@ -1118,12 +1269,12 @@
     gain_first = jnp.sum(spread[:64], axis=0, keepdims=True)
     gain_ref[0:1, :] = gain_first
     gain_ref[1:2, :] = jnp.sum(spread[64:], axis=0, keepdims=True)
-    normed = (start_ref[...] * scale_ref[...] * gain_first).astype(jnp.bfloat16)
+    start = start_ref[...]
+    normed = (start * norm_scale(start) * gain_first).astype(jnp.bfloat16)
     n_ref[...] = normed
-    projected = dot(normed, w_ref[...])
-    natural = jnp.concatenate(
-        [projected[:, :IN_HALF], projected[:, IN_PAD : IN_PAD + IN_HALF]], axis=1
-    )
+    for copy in loads:
+        copy.wait()
+    natural = jnp.concatenate([dot(normed, weight[k])[:, :IN_HALF] for k in range(2)], axis=1)
     key_width = KEY_VALUE_HEADS * HEAD_SIZE
     turned = rotate_tiles(natural[:, : WIDTH + key_width], cos_ref[...], sin_ref[...])
     q_ref[...] = turned[:, :WIDTH].astype(jnp.bfloat16) * jnp.bfloat16(0.125)
@@ -1135,16 +1286,22 @@
     kv_ref[...] = jnp.concatenate(pieces, axis=1).astype(jnp.bfloat16)
 
 
-def local_call(kernel, shapes, flops):
+def local_call(kernel, shapes, operands, weights, flops):
     return pl.pallas_call(
         kernel,
         out_shape=tuple(jax.ShapeDtypeStruct(shape, kind) for shape, kind in shapes),
+        in_specs=[pl.BlockSpec(memory_space=pltpu.VMEM)] * len(operands)
+        + [pl.BlockSpec(memory_space=pl.ANY)],
+        scratch_shapes=[
+            pltpu.VMEM((2, PADDED, IN_PAD), jnp.bfloat16),
+            pltpu.SemaphoreType.DMA((2,)),
+        ],
         compiler_params=pltpu.CompilerParams(vmem_limit_bytes=VMEM_LIMIT),
         cost_estimate=pl.CostEstimate(flops=flops, bytes_accessed=6 * 10**6, transcendentals=0),
-    )
-
-
-def project(start, scale, spare, weight, cosine, sine):
+    )(*operands, weights)
+
+
+def project(start, spare, cosine, sine, weights):
     low, full = jnp.bfloat16, jnp.float32
     shapes = (
         ((128, PADDED), low),
@@ -1152,24 +1309,34 @@
         ((128, 2 * KEY_VALUE_HEADS * HEAD_SIZE), low),
         ((2, PADDED), full),
     )
-    return local_call(project_kernel, shapes, 5 * 10**8)(start, scale, spare, weight, cosine, sine)
+    return local_call(project_kernel, shapes, (start, spare, cosine, sine), weights, 5 * 10**8)
 
 
 def project_back_kernel(
     dq_ref,
     kv_ref,
     start_ref,
-    scale_ref,
     gain_ref,
     gain_two_ref,
-    resid_ref,
+    resid_grad_ref,
     n_ref,
-    w_ref,
     cos_ref,
     sin_ref,
+    resid_ref,
+    ffn_ref,
+    map_ref,
+    w_hbm,
     grad_ref,
+    layer_ref,
     input_ref,
+    weight,
+    w_sems,
 ):
+    loads = load_halves(w_hbm, weight, w_sems, 0)
+    row = lax.broadcasted_iota(jnp.int32, (WIDTH, PADDED), 0)
+    select = jnp.where(row == map_ref[...], 1.0, 0.0).astype(jnp.bfloat16)
+    layer = (resid_ref[...] + ffn_ref[...]).astype(jnp.bfloat16)
+    layer_ref[...] = dot(select, layer, LAST).astype(jnp.bfloat16)
     key_width = KEY_VALUE_HEADS * HEAD_SIZE
     kv = kv_ref[...]
     keys = [kv[:, g * 128 : g * 128 + 64] for g in range(KEY_VALUE_HEADS)]
@@ -1180,11 +1347,15 @@
     natural = jnp.concatenate([turned] + values, axis=1).astype(jnp.bfloat16)
     blank = jnp.zeros((128, IN_PAD - IN_HALF), jnp.bfloat16)
     grads = jnp.concatenate([natural[:, :IN_HALF], blank, natural[:, IN_HALF:], blank], axis=1)
-    back = dot(grads, w_ref[...], LAST)
-    start, scale = start_ref[...], scale_ref[...]
+    for copy in loads:
+        copy.wait()
+    back = dot(grads[:, :IN_PAD], weight[0], LAST) + dot(grads[:, IN_PAD:], weight[1], LAST)
+    start = start_ref[...]
+    scale = norm_scale(start)
     gain_grad = jnp.sum(back * start * scale, axis=0, keepdims=True)
     through = norm_backward(start, scale, back * gain_ref[0:1, :])
-    input_ref[...] = (resid_ref[...] + through).astype(jnp.bfloat16)
+    change = (resid_grad_ref[...] + through).astype(jnp.bfloat16)
+    input_ref[...] = dot(select, change, LAST).astype(jnp.bfloat16)
     for k in range(PADDED // 256):
         span = slice(k * 256, k * 256 + 256)
         grad_ref[span, :] = dot(n_ref[:, span], grads, FIRST).astype(jnp.bfloat16)
@@ -1203,9 +1374,24 @@
         grad_ref[:, span] = grad_ref[:, span] + dot(place, by_slot).astype(jnp.bfloat16)
 
 
-def project_back(*operands):
-    shapes = (((PADDED, IN_COLS), jnp.bfloat16), ((128, PADDED), jnp.bfloat16))
-    return local_call(project_back_kernel, shapes, 10**9)(*operands)
+def project_back(operands, weights):
+    low = jnp.bfloat16
+    shapes = (((PADDED, IN_COLS), low), ((WIDTH, 128), low), ((WIDTH, 128), low))
+    return local_call(project_back_kernel, shapes, operands, weights, 10**9)
+
+
+def store_kernel(*refs):
+    count = len(refs) // 2
+    for source, place in zip(refs[:count], refs[count:]):
+        place[...] = source[...]
+
+
+def store(arrays):
+    return pl.pallas_call(
+        store_kernel,
+        out_shape=tuple(jax.ShapeDtypeStruct(array.shape, array.dtype) for array in arrays),
+        compiler_params=pltpu.CompilerParams(vmem_limit_bytes=VMEM_LIMIT),
+    )(*arrays)
 
 
 def on_device(
@@ -1227,36 +1413,23 @@
     ).astype(jnp.bfloat16)
 
     spare = jnp.pad(norm_gains.T, ((0, 0), (0, 1)))
-    own_in = pad_columns(
-        jnp.concatenate([input_projection, pad_columns(spare, IN_HALF)], axis=0), IN_PAD
-    )
+    own_in = jnp.concatenate([input_projection, pad_columns(spare, IN_HALF)], axis=0)
     own_in = own_in.at[15, ROWS].set(pair.astype(jnp.bfloat16))
     own_out = jnp.pad(project_out, ((0, 1), (0, OUT_PAD - OUT_HALF)))
-    gate_up_parts = gate_up.reshape(15, 2, 2, FF_QUARTER).transpose(2, 0, 1, 3)
-    gate_up_parts = gate_up_parts.reshape(2, 15, 2 * FF_QUARTER)
-    down_parts = down_weight.reshape(15, 2, FF_QUARTER).transpose(1, 0, 2)
-    spare_row = ((0, 0), (0, 1), (0, 0))
+    own_att = jnp.concatenate([pad_columns(own_in, IN_PAD), own_out], axis=1)
+    parts = jnp.concatenate([gate_up, down_weight[:, None]], axis=1)
+    parts = parts.reshape(15, 3, 2, FF_QUARTER).transpose(2, 0, 1, 3)
+    parts = jnp.pad(parts.reshape(2, 15, 3 * FF_QUARTER), ((0, 0), (0, 1), (0, 0)))
     upstream = dot(cotangent[0], select)
-    weight_in, weight_out, weight_gu, weight_down, row_cotangent = gather_blocks(
-        (
-            own_in,
-            own_out,
-            jnp.pad(gate_up_parts, spare_row),
-            jnp.pad(down_parts, spare_row),
-        ),
-        ("row", "row", "split", "split"),
-        upstream.astype(jnp.bfloat16),
-        0,
-    )
-    weight_in = weight_in.reshape(PADDED, IN_COLS)
-    weight_out = weight_out.reshape(PADDED, 2 * OUT_PAD)
-    weight_gu = weight_gu.reshape(PADDED, 2 * FF_QUARTER)
-    weight_down = weight_down.reshape(PADDED, FF_QUARTER)
+    weight_att, weight_ffn, row_cotangent = gather_blocks(
+        (own_att, parts, upstream.astype(jnp.bfloat16)), 0
+    )
+    weight_att = weight_att.reshape(PADDED, 2 * (IN_PAD + OUT_PAD))
+    weight_ffn = weight_ffn.reshape(PADDED, 3 * FF_QUARTER)
     row_cotangent = row_cotangent.reshape(512, PADDED)
-    blocks_in = weight_in.reshape(64, ROWS, IN_COLS)
-    spare_first = blocks_in[:, 15, : 2 * ROWS]
-    spare_second = blocks_in[:, 15, IN_PAD : IN_PAD + 2 * ROWS]
-    held = jnp.arange(PADDED) % ROWS < 15
+    blocks_att = weight_att.reshape(64, ROWS, 2 * (IN_PAD + OUT_PAD))
+    spare_first = blocks_att[:, 15, : 2 * ROWS]
+    spare_second = blocks_att[:, 15, IN_PAD + OUT_PAD : IN_PAD + OUT_PAD + 2 * ROWS]
     labels = jnp.where(half == 0, spare_first, spare_second)[:, ROWS].astype(jnp.int32)
     slots = jnp.arange(64, dtype=jnp.int32)
     blocks = jnp.stack([labels, 127 - labels], axis=1).reshape(128)
@@ -1272,32 +1445,31 @@
     cosine = jnp.tile(jnp.cos(angle), (1, 4))
     sine = jnp.sin(angle)
     sine = jnp.tile(jnp.concatenate([-sine, sine], axis=1), (1, 2))
-    scale_one = lax.rsqrt(jnp.sum(start * start, axis=-1, keepdims=True) / WIDTH + EPSILON)
     spare = jnp.concatenate([spare_first[:, :ROWS], spare_second[:, :ROWS]], axis=0)
     normed_low, query_scaled, key_value, gains = project(
-        start, scale_one, spare, weight_in, cosine, sine
-    )
-    gain_second = gains[1]
-    all_kv = gather_blocks((key_value,), ("whole",), None, 1)[0].reshape(128, 64, 2 * key_width)
+        start, spare, cosine, sine, weight_att
+    )
+    all_kv = gather_blocks((key_value,), 1)[0].reshape(128, 64, 2 * key_width)
     pair_one = pair.reshape(1)
-    attention, top, total = attend(table, pair_one, query_scaled, all_kv)
-    mixed_low = pad_halves(attention.astype(jnp.bfloat16), OUT_HALF, OUT_PAD)
-    branch = dot(mixed_low, weight_out, LAST)
-    resid = start + jnp.where(held, branch, 0.0)
-    scale_two = lax.rsqrt(jnp.sum(resid * resid, axis=-1, keepdims=True) / WIDTH + EPSILON)
-    normed_two = (resid * scale_two * gain_second).astype(jnp.bfloat16)
+    attention, top, total, mixed_low, resid, normed_two = attend(
+        table, pair_one, query_scaled, start, gains, all_kv, weight_att
+    )
     normed_two_grad, ffn_out, grad_gu, grad_down = feed_forward(
-        normed_two, row_cotangent, weight_gu, weight_down, 2
-    )
-    resid_grad = upstream + norm_backward(resid, scale_two, normed_two_grad * gain_second)
-    gain_two_grad = jnp.sum(normed_two_grad * resid * scale_two, axis=0, keepdims=True)
-    branch_grad_low = resid_grad.astype(jnp.bfloat16)
-    mixed_grad = dot(branch_grad_low, weight_out)
-    mixed_grad = jnp.concatenate(
-        [mixed_grad[:, :OUT_HALF], mixed_grad[:, OUT_PAD : OUT_PAD + OUT_HALF]], axis=1
-    )
-    query_grad, all_kv_grad = attend_back(
-        table, pair_one, query_scaled, mixed_grad, attention, top, total, all_kv
+        normed_two, row_cotangent, weight_ffn, 2
+    )
+    query_grad, all_kv_grad, resid_grad, branch_grad_low, gain_two_grad = attend_back(
+        table,
+        pair_one,
+        query_scaled,
+        normed_two_grad,
+        resid,
+        upstream,
+        gains,
+        attention,
+        top,
+        total,
+        all_kv,
+        weight_att,
     )
     kv_grad, ffn_out, grad_out = scatter_blocks(
         (all_kv_grad.reshape(2, 4, 4, 2, 128, 2 * key_width),),
@@ -1311,23 +1483,25 @@
         ),
         3,
     )
-    layer_out = (resid + ffn_out).astype(jnp.bfloat16)
-    grad_in, input_grad = project_back(
-        query_grad,
-        kv_grad,
-        start,
-        scale_one,
-        gains,
-        gain_two_grad,
-        resid_grad,
-        normed_low,
-        weight_in,
-        cosine,
-        sine,
+    grad_in, layer_out, input_grad = project_back(
+        (
+            query_grad,
+            kv_grad,
+            start,
+            gains,
+            gain_two_grad,
+            resid_grad,
+            normed_low,
+            cosine,
+            sine,
+            resid,
+            ffn_out,
+            jnp.asarray(COLUMN_MAP)[None, :],
+        ),
+        weight_att,
     )
     own_cols = IN_PAD + OUT_PAD
-    narrow = jax.ShapeDtypeStruct((WIDTH, 128), jnp.bfloat16)
-    sum_in, sum_out, sum_gu, sum_down, spare, layer_out, input_grad = scatter_blocks(
+    sums = scatter_blocks(
         tuple(
             grad.reshape(2, 4, 4, 2, ROWS, grad.shape[1])
             for grad in (grad_in, grad_out, grad_gu, grad_down)
@@ -1342,9 +1516,10 @@
         ),
         own_cols,
         None,
-        (unpad_work, (layer_out, input_grad, select), (narrow, narrow)),
+        (lambda ins, outs: None, (), ()),
         4,
     )
+    sum_in, sum_out, sum_gu, sum_down, spare = store(sums)
     return (
         layer_out.T[None],
         input_grad.T[None],

time: 327 us -> 292 us (0.89)
  Pallas kernels: 288 us -> 274 us
  local copies, waits for them, and re-layouts: 18.3 us -> 6.82 us
  other arithmetic: 13.1 us -> 4.74 us
    pallas_call x4 -> x5, Pallas kernels: 110 us -> 93.9 us  [the longest x2 76.9 us: gather_blocks(): pl.pallas_call(lambda *refs: gather_kernel(len(blocks), *refs), out_shape...]
    unnamed x32 -> x6, local copies, waits for them, and re-layouts: 9.46 us -> 0.18 us
    convert_element_type x5 -> x0, other arithmetic: 7.85 us -> none  [the longest x1 2.09 us: on_device(): branch_grad_low = resid_grad.astype(jnp.bfloat16)]
where the time goes in v2:
time: 292 us; the launch traced here: 291 us
  Pallas kernels  274 us (94%)
  local copies, waits for them, and re-layouts  6.82 us (2%)
  other arithmetic  4.74 us (2%)
  matrix products  4.31 us (1%)
    pallas_call x2, Pallas kernels, scatter_blocks(): pl.pallas_call(lambda *refs: scatter_kernel(pieces, halved, with_row, sid...  94.8 us
    pallas_call x2, Pallas kernels, gather_blocks(): pl.pallas_call(lambda *refs: gather_kernel(len(blocks), *refs), out_shape...  76.9 us
    pallas_call x1, Pallas kernels, feed_forward(): pl.pallas_call(feed_forward_kernel, out_shape=(jax.ShapeDtypeStruct((128,...  33.4 us
    pallas_call x1, Pallas kernels, attend_back(): pl.pallas_call(attend_back_kernel, out_shape=(jax.ShapeDtypeStruct((128,...  31.6 us
    pallas_call x1, Pallas kernels, attend(): pl.pallas_call(attend_kernel, out_shape=(jax.ShapeDtypeStruct((128, WIDTH...  19.8 us
    pallas_call x2, Pallas kernels, local_call(): pl.pallas_call(kernel, out_shape=tuple((jax.ShapeDtypeStruct(shape, kind)...  15.2 us

profile of v2, /device:TPU:0, one launch (start us, length us, event | category | flops | bytes accessed | tf_op | source)
XLA Modules:
  0.0 290.9 jit_solution(11732862557345834462)
XLA Ops:
  1.4 0.7 convert_bitcast_fusion
  2.0 0.8 fusion.12
  2.9 1.3 fusion.11.refs_0_
  4.7 0.7 copy.57.sin_ref
  5.4 0.7 copy.56.cos_ref
  6.2 0.9 concatenate.29
  7.0 1.1 maximum_bitcast_fusion
  8.3 0.7 pad.28.refs_1_
  8.9 2.6 fusion.5.start_ref
  11.5 1.7 fusion.17
  13.3 39.7 %shard_map.153 = (bf16[2,4,4,2,16,2816]{5,4,3,2,1,0:T(8,128)(2,1)}, bf16[2,4,4,2,16,1920]{5,4,3,2,1,0:T(8,128)(2,1)}, bf16[4,128,1024]{2,1,0:T(8,128)(2,1)}) custom-call(bf16[16,1408]{1,0:T(8,128)(2,1)} %fusion.11.refs_0_, bf16[2,16,1920]{2,1,0:T(8,128)(2,1)} %pad.28.refs_1_, bf16[128,1024]{1,0:T(8,128)(2,1)} %get-tuple-element.102.refs_2_), custom_call_target="tpu_custom_call" | custom-call | tf_op jit(solution)/shard_map/pallas_call | solution.py:419
  53.0 1.0 fusion.16
  54.3 0.7 copy.55.spare_ref
  55.3 0.6 select_reduce_fusion.table_ref
  55.9 4.8 %shard_map.154 = (bf16[128,1024]{1,0:T(8,128)(2,1)}, bf16[128,960]{1,0:T(8,128)(2,1)}, bf16[128,640]{1,0:T(8,128)(2,1)}, f32[2,1024]{1,0:T(2,128)}) custom-call(f32[128,1024]{1,0:T(8,128)} %fusion.5.start_ref, bf16[128,16]{1,0:T(8,128)(2,1)} %copy.55.spare_ref, f32[128,128]{1,0:T(8,128)} %copy.56.cos_ref, f32[128,128]{1,0:T(8,128)} %copy.57.sin_ref, ...), custom_call_target="tpu_custom_call" | custom-call | flops 500000000 | bytes 6000000 | tf_op jit(solution)/shard_map/pallas_call | solution.py:1290
  60.7 37.2 %shard_map.155 = bf16[2,4,4,2,128,640]{5,4,3,2,1,0:T(8,128)(2,1)} custom-call(bf16[128,640]{1,0:T(8,128)(2,1)} %get-tuple-element.60.refs_0_), custom_call_target="tpu_custom_call" | custom-call | tf_op jit(solution)/shard_map/pallas_call | solution.py:419
  97.9 19.8 %shard_map.156 = (f32[128,960]{1,0:T(8,128)}, f32[5,384,128]{2,1,0:T(8,128)}, f32[5,384,128]{2,1,0:T(8,128)}, bf16[128,1024]{1,0:T(8,128)(2,1)}, f32[128,1024]{1,0:T(8,128)}, /*index=5*/bf16[128,1024]{1,0:T(8,128)(2,1)}) custom-call(s32[128]{0:T(128)} %select_reduce_fusion.table_ref, s32[1]{0:T(128)} %bitcast.44.pair_ref, ...), custom_call_target="tpu_custom_call" | custom-call | flops 4000000000 | bytes 10000000 | tf_op jit(solution)/shard_map/pallas_call | solution.py:1035
  117.7 33.4 %shard_map.157 = (f32[128,1024]{1,0:T(8,128)}, bf16[512,1024]{1,0:T(8,128)(2,1)}, bf16[1024,1280]{1,0:T(8,128)(2,1)}, bf16[1024,640]{1,0:T(8,128)(2,1)}) custom-call(bf16[128,1024]{1,0:T(8,128)(2,1)} %get-tuple-element.61.n_ref, bf16[512,1024]{1,0:T(8,128)(2,1)} %bitcast.68, bf16[1024,1920]{1,0:T(8,128)(2,1)} %bitcast.67), custom_call_target="tpu_custom_call" | custom-call | flops 7000000000 | bytes 10000000 | tf_op jit(solution)/shard_map/pallas_call | solution.py:842
  151.2 31.6 %shard_map.158 = (f32[128,960]{1,0:T(8,128)}, bf16[128,64,640]{2,1,0:T(8,128)(2,1)}, f32[128,1024]{1,0:T(8,128)}, bf16[128,1024]{1,0:T(8,128)(2,1)}, f32[1,1024]{1,0:T(1,128)}) custom-call(s32[128]{0:T(128)} %select_reduce_fusion.table_ref, s32[1]{0:T(128)} %bitcast.45.pair_ref, bf16[128,960]{1,0:T(8,128)(2,1)} %get-tuple-element.58.q_ref, ...), custom_call_target="tpu_custom_call" | custom-call | flops 10000000000 | bytes 20000000 | tf_op jit(solution)/shard_map/pallas_call | solution.py:1185
  182.8 48.5 %shard_map.159 = (f32[128,640]{1,0:T(8,128)}, f32[128,1024]{1,0:T(8,128)}, bf16[1024,1024]{1,0:T(8,128)(2,1)}) custom-call(bf16[2,4,4,2,128,640]{5,4,3,2,1,0:T(8,128)(2,1)} %bitcast.53, bf16[4,128,1024]{2,1,0:T(8,128)(2,1)} %bitcast.58, bf16[128,1024]{1,0:T(8,128)(2,1)} %get-tuple-element.72.refs_2_, bf16[128,1024]{1,0:T(8,128)(2,1)} %get-tuple-element.73.refs_3_), custom_call_target="tpu_custom_call" | custom-call | tf_op jit(solution)/shard_map/pallas_call | solution.py:662
  231.3 10.4 %shard_map.160 = (bf16[1024,1792]{1,0:T(8,128)(2,1)}, bf16[960,128]{1,0:T(8,128)(2,1)}, bf16[960,128]{1,0:T(8,128)(2,1)}) custom-call(f32[128,960]{1,0:T(8,128)} %get-tuple-element.69.dq_ref, f32[128,640]{1,0:T(8,128)} %get-tuple-element.74.kv_ref, f32[128,1024]{1,0:T(8,128)} %fusion.5.start_ref, f32[2,1024]{1,0:T(2,128)} %get-tuple-element.59.gain_ref, ...), custom_call_target="tpu_custom_call" | custom-call | flops 1000000000 | bytes 6000000 | tf_op jit(solution)/shard_map/pallas_call | solution.py:1290
  241.8 46.2 %shard_map.161 = (f32[15,800]{1,0:T(8,128)}, f32[15,480]{1,0:T(8,128)}, f32[15,2,1280]{2,1,0:T(2,128)}, f32[15,1280]{1,0:T(8,128)}, f32[1,128]{1,0:T(1,128)}) custom-call(bf16[2,4,4,2,16,1792]{5,4,3,2,1,0:T(8,128)(2,1)} %bitcast.54, bf16[2,4,4,2,16,1024]{5,4,3,2,1,0:T(8,128)(2,1)} %bitcast.56, bf16[2,4,4,2,16,1280]{5,4,3,2,1,0:T(8,128)(2,1)} %bitcast.55, ...), custom_call_target="tpu_custom_call" | custom-call | tf_op jit(solution)/shard_map/pallas_call | solution.py:662
  288.0 1.7 shard_map.162
  289.8 1.1 slice_bitcast_fusion
  (25 shorter events, 1.2 us)
Async XLA Ops:
  0.6 10.9 %copy-start = (bf16[1,128,960]{1,2,0:T(8,128)(2,1)S(1)}, bf16[1,128,960]{1,2,0:T(8,128)(2,1)}, u32[]{:S(2)}) copy-start(bf16[1,128,960]{1,2,0:T(8,128)(2,1)} %param.13) | copy-start | bytes 737284
  0.6 10.9 %copy-start.1 = (s32[1024]{0:T(1024)S(1)}, s32[1024]{0:T(1024)}, u32[]{:S(2)}) copy-start(s32[1024]{0:T(1024)} %constant.55.clone) | copy-start | bytes 12292

commit v3 on v2

--- a/solution.py
+++ b/solution.py
@@ -74,12 +74,6 @@
 def half_of(ref, core, x, p2):
     every = pl.ds(0, 4)
     return ref.at[x, every, p2, core] if core == 0 else ref.at[x, p2, every, core]
-
-
-def slab_of(ref, core, p2):
-    every = pl.ds(0, 4)
-    both = pl.ds(0, 2)
-    return ref.at[both, every, p2, core] if core == 0 else ref.at[both, p2, every, core]
 
 
 def row_place():
@@ -459,41 +453,42 @@
     theirs = (p1o, p1m, p1p, p1)
     sender = Sender(send_sem, recv_sem)
 
-    def part(ref, place, piece):
+    def part(ref, place, side, piece):
         if len(pieces) == 1:
-            return ref.at[place]
-        every = [pl.ds(0, size) for size in ref.shape[1:-1]]
-        return ref.at[tuple([place] + every + [pl.ds(pieces[piece][3], pieces[piece][2])])]
-
-    def source_of(piece, chosen, place):
+            return ref.at[place, side]
+        every = [pl.ds(0, size) for size in ref.shape[2:-1]]
+        return ref.at[tuple([place, side] + every + [pl.ds(pieces[piece][3], pieces[piece][2])])]
+
+    def source_of(piece, chosen, place, side):
         array, start, width, _ = pieces[piece]
-        slab = slab_of(ins[array], chosen, place)
+        half = half_of(ins[array], chosen, side, place)
         if len(pieces) == 1:
-            return slab
-        every = [pl.ds(0, size) for size in slab.shape[:-1]]
-        return slab.at[tuple(every + [pl.ds(start, width)])]
-
-    def crossing(k, piece, source):
+            return half
+        every = [pl.ds(0, size) for size in half.shape[:-1]]
+        return half.at[tuple(every + [pl.ds(start, width)])]
+
+    def crossing(k, side, piece, source):
         return pltpu.make_async_remote_copy(
             src_ref=source,
-            dst_ref=part(other, theirs[k], piece),
-            send_sem=cross_send.at[k, piece],
-            recv_sem=cross_recv.at[k, piece],
+            dst_ref=part(other, theirs[k], side, piece),
+            send_sem=cross_send.at[2 * k + side, piece],
+            recv_sem=cross_recv.at[2 * k + side, piece],
             device_id=ctx_device(sibling),
             device_id_type=MESH,
         )
 
+    order = ((0, 0), (0, 1), (1, 0), (2, 1), (2, 0), (1, 1), (3, 0), (3, 1))
     for chosen in range(2):
 
         @pl.when(core == chosen)
         def _(chosen=chosen):
-            for k in range(4):
+            for k, side in order:
                 for piece in range(len(pieces)):
-                    crossing(k, piece, source_of(piece, 1 - chosen, theirs[k])).start()
+                    crossing(k, side, piece, source_of(piece, 1 - chosen, theirs[k], side)).start()
                     pltpu.make_async_copy(
-                        source_of(piece, chosen, needed[k]),
-                        part(acc, needed[k], piece),
-                        local_sem.at[k, piece],
+                        source_of(piece, chosen, needed[k], side),
+                        part(acc, needed[k], side, piece),
+                        local_sem.at[2 * k + side, piece],
                     ).start()
 
     if with_row:
@@ -508,61 +503,75 @@
         def _(step):
             place[step] = place[step] + term[step]
 
-    def add_both(side):
-        @pl.loop(0, 4)
-        def _(step):
-            total = acc[p2, side, step].astype(jnp.float32)
-            total = total + near_left[side, step].astype(jnp.float32)
-            total = total + near_right[side, step].astype(jnp.float32)
-            acc[p2, side, step] = total.astype(acc.dtype)
-
-    def merge(k):
+    def total(side, q1):
+        value = acc[p2, side, q1].astype(jnp.float32)
+        value = value + near_left[side, q1].astype(jnp.float32)
+        value = value + near_right[side, q1].astype(jnp.float32)
+        acc[p2, side, q1] = value.astype(acc.dtype)
+
+    def merge(k, side):
         for piece in range(len(pieces)):
-            mine = part(acc, needed[k], piece)
-            pltpu.make_async_copy(mine, mine, local_sem.at[k, piece]).wait()
-            crossing(k, piece, part(other, theirs[k], piece)).wait_recv()
-        for side in range(2):
-            add(acc.at[needed[k], side], other.at[needed[k], side])
-
-    merge(0)
+            mine = part(acc, needed[k], side, piece)
+            pltpu.make_async_copy(mine, mine, local_sem.at[2 * k + side, piece]).wait()
+            crossing(k, side, piece, part(other, theirs[k], side, piece)).wait_recv()
+        add(acc.at[needed[k], side], other.at[needed[k], side])
+
+    merge(0, 0)
     got_low = send(acc.at[p2o, 0], far_low, right2)
+    merge(0, 1)
     got_high = send(acc.at[p2o, 1], far_high, left2)
-    merge(1)
+    merge(1, 0)
     right_low = send(acc.at[p2m, 0], near_right.at[0], left2)
-    merge(2)
+    merge(2, 1)
     left_high = send(acc.at[p2p, 1], near_left.at[1], right2)
     side_work(side_ins, side_outs)
+    merge(2, 0)
+    merge(1, 1)
+    turns = (p1o, p1m, p1p, p1)
     got_low.wait_recv()
     add(acc.at[p2p, 0], far_low)
-    left_low = send(acc.at[p2p, 0], near_left.at[0], right2)
+    left_low = [send(acc.at[p2p, 0, q1], near_left.at[0, q1], right2) for q1 in turns]
     got_high.wait_recv()
     add(acc.at[p2m, 1], far_high)
-    right_high = send(acc.at[p2m, 1], near_right.at[1], left2)
-    merge(3)
+    right_high = [send(acc.at[p2m, 1, q1], near_right.at[1, q1], left2) for q1 in turns]
+    merge(3, 0)
+    merge(3, 1)
     if with_row:
         row.forward()
     right_low.wait_recv()
-    left_low.wait_recv()
-    add_both(0)
+    left_high.wait_recv()
+    left_low[0].wait_recv()
+    total(0, p1o)
     got_low = send(acc.at[p2, 0, p1o], pair_low, right1)
+    right_high[0].wait_recv()
+    total(1, p1o)
+    got_high = send(acc.at[p2, 1, p1o], pair_high, left1)
+    left_low[1].wait_recv()
+    total(0, p1m)
     near_low = send(acc.at[p2, 0, p1m], pair_right.at[0], left1)
-    left_high.wait_recv()
-    right_high.wait_recv()
-    add_both(1)
-    got_high = send(acc.at[p2, 1, p1o], pair_high, left1)
+    right_high[1].wait_recv()
+    total(1, p1m)
+    right_high[2].wait_recv()
+    total(1, p1p)
     near_high = send(acc.at[p2, 1, p1p], pair_left.at[1], right1)
+    left_low[2].wait_recv()
+    total(0, p1p)
     got_low.wait_recv()
     acc[p2, 0, p1p] = acc[p2, 0, p1p] + pair_low[...]
-    left_low = send(acc.at[p2, 0, p1p], pair_left.at[0], right1)
+    pair_first = send(acc.at[p2, 0, p1p], pair_left.at[0], right1)
     got_high.wait_recv()
     acc[p2, 1, p1m] = acc[p2, 1, p1m] + pair_high[...]
-    right_high = send(acc.at[p2, 1, p1m], pair_right.at[1], left1)
+    pair_second = send(acc.at[p2, 1, p1m], pair_right.at[1], left1)
+    left_low[3].wait_recv()
+    total(0, p1)
+    right_high[3].wait_recv()
+    total(1, p1)
     if with_row:
         row.finish(row_out)
     near_low.wait_recv()
     near_high.wait_recv()
-    left_low.wait_recv()
-    right_high.wait_recv()
+    pair_first.wait_recv()
+    pair_second.wait_recv()
 
     @pl.loop(0, 2)
     def _(j):
@@ -577,9 +586,9 @@
         final.wait_recv()
         total = acc[p2, x, p1].astype(jnp.float32) + last[...].astype(jnp.float32)
         out_refs[0][...] = total
-    for k in range(4):
+    for k, side in order:
         for piece in range(len(pieces)):
-            crossing(k, piece, part(other, theirs[k], piece)).wait_send()
+            crossing(k, side, piece, part(other, theirs[k], side, piece)).wait_send()
     sender.finish()
     if with_row:
         row_sender.finish()
@@ -676,11 +685,11 @@
             pltpu.VMEM((2,) + block, kind),
             pltpu.VMEM((2,) + block, kind),
             pltpu.VMEM(last, kind),
-            pltpu.SemaphoreType.DMA((4, len(pieces))),
-            pltpu.SemaphoreType.DMA((4, len(pieces))),
-            pltpu.SemaphoreType.DMA((4, len(pieces))),
-            pltpu.SemaphoreType.DMA((16,)),
-            pltpu.SemaphoreType.DMA((16,)),
+            pltpu.SemaphoreType.DMA((8, len(pieces))),
+            pltpu.SemaphoreType.DMA((8, len(pieces))),
+            pltpu.SemaphoreType.DMA((8, len(pieces))),
+            pltpu.SemaphoreType.DMA((24,)),
+            pltpu.SemaphoreType.DMA((24,)),
         ]
         + scratch,
         compiler_params=pltpu.CompilerParams(

time: 292 us -> 286 us (0.979)
  Pallas kernels: 274 us -> 267 us
    pallas_call x2, Pallas kernels: 94.8 us -> 86.1 us  [scatter_blocks(): pl.pallas_call(lambda *refs: scatter_kernel(pieces, halved, with_row, sid...]
where the time goes in v3:
time: 286 us; the launch traced here: 285 us
  Pallas kernels  267 us (93%)
  local copies, waits for them, and re-layouts  6.82 us (2%)
  other arithmetic  4.74 us (2%)
  matrix products  4.31 us (2%)
    pallas_call x2, Pallas kernels, scatter_blocks(): pl.pallas_call(lambda *refs: scatter_kernel(pieces, halved, with_row, sid...  86.1 us
    pallas_call x2, Pallas kernels, gather_blocks(): pl.pallas_call(lambda *refs: gather_kernel(len(blocks), *refs), out_shape...  76.9 us
    pallas_call x1, Pallas kernels, feed_forward(): pl.pallas_call(feed_forward_kernel, out_shape=(jax.ShapeDtypeStruct((128,...  34.5 us
    pallas_call x1, Pallas kernels, attend_back(): pl.pallas_call(attend_back_kernel, out_shape=(jax.ShapeDtypeStruct((128,...  32.1 us
    pallas_call x1, Pallas kernels, attend(): pl.pallas_call(attend_kernel, out_shape=(jax.ShapeDtypeStruct((128, WIDTH...  20.5 us
    pallas_call x2, Pallas kernels, local_call(): pl.pallas_call(kernel, out_shape=tuple((jax.ShapeDtypeStruct(shape, kind)...  15.2 us

profile of v3, /device:TPU:0, one launch (start us, length us, event | category | flops | bytes accessed | tf_op | source)
XLA Modules:
  0.0 284.5 jit_solution(4058508001552153591)
XLA Ops:
  1.4 0.7 convert_bitcast_fusion
  2.0 0.8 fusion.12
  2.9 1.3 fusion.11.refs_0_
  4.7 0.7 copy.57.sin_ref
  5.4 0.7 copy.56.cos_ref
  6.2 0.9 concatenate.29
  7.0 1.1 maximum_bitcast_fusion
  8.3 0.7 pad.28.refs_1_
  8.9 2.6 fusion.5.start_ref
  11.5 1.7 fusion.17
  13.3 39.7 %shard_map.153 = (bf16[2,4,4,2,16,2816]{5,4,3,2,1,0:T(8,128)(2,1)}, bf16[2,4,4,2,16,1920]{5,4,3,2,1,0:T(8,128)(2,1)}, bf16[4,128,1024]{2,1,0:T(8,128)(2,1)}) custom-call(bf16[16,1408]{1,0:T(8,128)(2,1)} %fusion.11.refs_0_, bf16[2,16,1920]{2,1,0:T(8,128)(2,1)} %pad.28.refs_1_, bf16[128,1024]{1,0:T(8,128)(2,1)} %get-tuple-element.102.refs_2_), custom_call_target="tpu_custom_call" | custom-call | tf_op jit(solution)/shard_map/pallas_call | solution.py:413
  53.0 1.0 fusion.16
  54.3 0.7 copy.55.spare_ref
  55.3 0.6 select_reduce_fusion.table_ref
  55.9 4.8 %shard_map.154 = (bf16[128,1024]{1,0:T(8,128)(2,1)}, bf16[128,960]{1,0:T(8,128)(2,1)}, bf16[128,640]{1,0:T(8,128)(2,1)}, f32[2,1024]{1,0:T(2,128)}) custom-call(f32[128,1024]{1,0:T(8,128)} %fusion.5.start_ref, bf16[128,16]{1,0:T(8,128)(2,1)} %copy.55.spare_ref, f32[128,128]{1,0:T(8,128)} %copy.56.cos_ref, f32[128,128]{1,0:T(8,128)} %copy.57.sin_ref, ...), custom_call_target="tpu_custom_call" | custom-call | flops 500000000 | bytes 6000000 | tf_op jit(solution)/shard_map/pallas_call | solution.py:1299
  60.7 37.2 %shard_map.155 = bf16[2,4,4,2,128,640]{5,4,3,2,1,0:T(8,128)(2,1)} custom-call(bf16[128,640]{1,0:T(8,128)(2,1)} %get-tuple-element.60.refs_0_), custom_call_target="tpu_custom_call" | custom-call | tf_op jit(solution)/shard_map/pallas_call | solution.py:413
  97.9 20.5 %shard_map.156 = (f32[128,960]{1,0:T(8,128)}, f32[5,384,128]{2,1,0:T(8,128)}, f32[5,384,128]{2,1,0:T(8,128)}, bf16[128,1024]{1,0:T(8,128)(2,1)}, f32[128,1024]{1,0:T(8,128)}, /*index=5*/bf16[128,1024]{1,0:T(8,128)(2,1)}) custom-call(s32[128]{0:T(128)} %select_reduce_fusion.table_ref, s32[1]{0:T(128)} %bitcast.44.pair_ref, ...), custom_call_target="tpu_custom_call" | custom-call | flops 4000000000 | bytes 10000000 | tf_op jit(solution)/shard_map/pallas_call | solution.py:1044
  118.5 34.5 %shard_map.157 = (f32[128,1024]{1,0:T(8,128)}, bf16[512,1024]{1,0:T(8,128)(2,1)}, bf16[1024,1280]{1,0:T(8,128)(2,1)}, bf16[1024,640]{1,0:T(8,128)(2,1)}) custom-call(bf16[128,1024]{1,0:T(8,128)(2,1)} %get-tuple-element.61.n_ref, bf16[512,1024]{1,0:T(8,128)(2,1)} %bitcast.68, bf16[1024,1920]{1,0:T(8,128)(2,1)} %bitcast.67), custom_call_target="tpu_custom_call" | custom-call | flops 7000000000 | bytes 10000000 | tf_op jit(solution)/shard_map/pallas_call | solution.py:851
  153.0 32.1 %shard_map.158 = (f32[128,960]{1,0:T(8,128)}, bf16[128,64,640]{2,1,0:T(8,128)(2,1)}, f32[128,1024]{1,0:T(8,128)}, bf16[128,1024]{1,0:T(8,128)(2,1)}, f32[1,1024]{1,0:T(1,128)}) custom-call(s32[128]{0:T(128)} %select_reduce_fusion.table_ref, s32[1]{0:T(128)} %bitcast.45.pair_ref, bf16[128,960]{1,0:T(8,128)(2,1)} %get-tuple-element.58.q_ref, ...), custom_call_target="tpu_custom_call" | custom-call | flops 10000000000 | bytes 20000000 | tf_op jit(solution)/shard_map/pallas_call | solution.py:1194
  185.1 43.8 %shard_map.159 = (f32[128,640]{1,0:T(8,128)}, f32[128,1024]{1,0:T(8,128)}, bf16[1024,1024]{1,0:T(8,128)(2,1)}) custom-call(bf16[2,4,4,2,128,640]{5,4,3,2,1,0:T(8,128)(2,1)} %bitcast.53, bf16[4,128,1024]{2,1,0:T(8,128)(2,1)} %bitcast.58, bf16[128,1024]{1,0:T(8,128)(2,1)} %get-tuple-element.72.refs_2_, bf16[128,1024]{1,0:T(8,128)(2,1)} %get-tuple-element.73.refs_3_), custom_call_target="tpu_custom_call" | custom-call | tf_op jit(solution)/shard_map/pallas_call | solution.py:671
  228.9 10.4 %shard_map.160 = (bf16[1024,1792]{1,0:T(8,128)(2,1)}, bf16[960,128]{1,0:T(8,128)(2,1)}, bf16[960,128]{1,0:T(8,128)(2,1)}) custom-call(f32[128,960]{1,0:T(8,128)} %get-tuple-element.69.dq_ref, f32[128,640]{1,0:T(8,128)} %get-tuple-element.74.kv_ref, f32[128,1024]{1,0:T(8,128)} %fusion.5.start_ref, f32[2,1024]{1,0:T(2,128)} %get-tuple-element.59.gain_ref, ...), custom_call_target="tpu_custom_call" | custom-call | flops 1000000000 | bytes 6000000 | tf_op jit(solution)/shard_map/pallas_call | solution.py:1299
  239.4 42.3 %shard_map.161 = (f32[15,800]{1,0:T(8,128)}, f32[15,480]{1,0:T(8,128)}, f32[15,2,1280]{2,1,0:T(2,128)}, f32[15,1280]{1,0:T(8,128)}, f32[1,128]{1,0:T(1,128)}) custom-call(bf16[2,4,4,2,16,1792]{5,4,3,2,1,0:T(8,128)(2,1)} %bitcast.54, bf16[2,4,4,2,16,1024]{5,4,3,2,1,0:T(8,128)(2,1)} %bitcast.56, bf16[2,4,4,2,16,1280]{5,4,3,2,1,0:T(8,128)(2,1)} %bitcast.55, ...), custom_call_target="tpu_custom_call" | custom-call | tf_op jit(solution)/shard_map/pallas_call | solution.py:671
  281.7 1.7 shard_map.162
  283.4 1.1 slice_bitcast_fusion
  (25 shorter events, 1.2 us)
Async XLA Ops:
  0.6 10.9 %copy-start = (bf16[1,128,960]{1,2,0:T(8,128)(2,1)S(1)}, bf16[1,128,960]{1,2,0:T(8,128)(2,1)}, u32[]{:S(2)}) copy-start(bf16[1,128,960]{1,2,0:T(8,128)(2,1)} %param.13) | copy-start | bytes 737284
  0.6 10.9 %copy-start.1 = (s32[1024]{0:T(1024)S(1)}, s32[1024]{0:T(1024)}, u32[]{:S(2)}) copy-start(s32[1024]{0:T(1024)} %constant.55.clone) | copy-start | bytes 12292
